TPU v7x, 32 devices: a whole 2x2x4 slice. The times are simulated.
32 devices in a mesh: dp: 8 (over z, y), mp: 4 (over x, core).
Axes of the slice: x: 2, y: 2, z: 4, core: 2. Of those that a mesh axis runs over, the one named last changes fastest.
Arguments:
- latents: float32 [8192, 16], P('dp'), may hold values from -6 to 6
- noise: float32 [8192, 16], P('dp'), may hold values from -6 to 6
- segment_ids: int32 [8192], P('dp'), may hold values from 0 to 3, as said below
- timesteps: int32 [8, 4], P('dp'), may hold values from 0 to 999
- labels: int32 [8, 4], P('dp'), may hold values from 0 to 1000
- w_qkv: float32 [768, 3, 768], P('dp', None, 'mp'), may hold values from -0.3125 to 0.3125
- w_out: float32 [768, 768], P('dp', 'mp'), may hold values from -0.625 to 0.625
- w_fc1: float32 [768, 3072], P('dp', 'mp'), may hold values from -0.21875 to 0.21875
- w_fc2: float32 [768, 3072], P('dp', 'mp'), may hold values from -0.109375 to 0.109375
- w_mod: float32 [768, 8, 768], P('dp', None, 'mp'), may hold values from -0.21875 to 0.21875
- w_head: float32 [768, 16], P('dp'), may hold values from -0.21875 to 0.21875
- w_cond: float32 [768, 2041], P('dp'), may hold values from -5 to 5
- mom_qkv: float32 [768, 3, 768], P('dp', None, 'mp'), may hold values from -0.00021362305 to 0.00021362305
- mom_out: float32 [768, 768], P('dp', 'mp'), may hold values from -0.00021362305 to 0.00021362305
- mom_fc1: float32 [768, 3072], P('dp', 'mp'), may hold values from -0.00021362305 to 0.00021362305
- mom_fc2: float32 [768, 3072], P('dp', 'mp'), may hold values from -0.00021362305 to 0.00021362305
- mom_mod: float32 [768, 8, 768], P('dp', None, 'mp'), may hold values from -0.00021362305 to 0.00021362305
- first_head: float32 [768, 16], P('dp'), may hold values from -2.2888184e-05 to 2.2888184e-05
- second_head: float32 [768, 16], P('dp'), may hold values from 9.718714e-12 to 3.9622448e-11
- first_cond: float32 [768, 2041], P('dp'), may hold values from -2.2888184e-05 to 2.2888184e-05
- second_cond: float32 [768, 2041], P('dp'), may hold values from 9.718714e-12 to 3.9622448e-11
Outputs:
- new_qkv: float32 [768, 3, 768], P('dp', None, 'mp')
- new_out: float32 [768, 768], P('dp', 'mp')
- new_fc1: float32 [768, 3072], P('dp', 'mp')
- new_fc2: float32 [768, 3072], P('dp', 'mp')
- new_mod: float32 [768, 8, 768], P('dp', None, 'mp')
- new_head: float32 [768, 16], P('dp')
- new_cond: float32 [768, 2041], P('dp')
- momentum_qkv: float32 [768, 3, 768], P('dp', None, 'mp')
- momentum_out: float32 [768, 768], P('dp', 'mp')
- momentum_fc1: float32 [768, 3072], P('dp', 'mp')
- momentum_fc2: float32 [768, 3072], P('dp', 'mp')
- momentum_mod: float32 [768, 8, 768], P('dp', None, 'mp')
- new_first_head: float32 [768, 16], P('dp')
- new_second_head: float32 [768, 16], P('dp')
- new_first_cond: float32 [768, 2041], P('dp')
- new_second_cond: float32 [768, 2041], P('dp')
- loss_sum: float32 [], replicated
- weight_total: float32 [], replicated
- grad_norm: float32 [], replicated
Inputs may be any that keep to these rules, and one draw needn't show every extreme that they name: `segment_ids`: each row of 1024 tokens is either one latent (all ids 0) or four latents of 256 tokens in order (ids 0, 1, 2, 3); at least one row holds four latents.
All inputs are finite; a program needn't handle non-finite values.
Results may differ from a plain program's by a relative error of at most 0.012.
Values may be sent and summed in bfloat16 or wider, within the bound.
No kernel may reach another device: no remote copies, remote signals or barrier semaphores. Data moves between devices by JAX's collectives and lax.ppermute only.
A program may use at most 256 MiB of HBM per device.

v0:
```python
import functools
import math

import jax
import jax.numpy as jnp
from jax import lax
from jax.experimental import pallas as pl
from jax.experimental.pallas import tpu as pltpu
from jax.sharding import PartitionSpec as P

SIDE = 32
D = 768
HEAD_DIM = 64
CLASSES = 1001
FREQ = 256
PIN = 16
STEP = 10
SLOTS = 4

HIGH = lax.Precision.HIGHEST
GAMMA = 5.0
CLIP = 0.05
MU = 0.95
LR_MUON = 0.1
DECAY = 0.01
BETA_ONE = 0.9
BETA_TWO = 0.95
LR_ADAM = 0.08
EPS_ADAM = 1e-08
NS_COEF = (3.4445, -4.775, 2.0315)
NS_SHIFT = (0.0, 0.1, 0.5, 0.8, 0.8)
ACROSS = (((1,), (1,)), ((), ()))
DOWN = (((0,), (0,)), ((), ()))
ALONG = (((1,), (0,)), ((), ()))
LOW = jnp.bfloat16
F32 = jnp.float32


def dot(a, b, dims=ALONG):
    return lax.dot_general(a, b, dims, preferred_element_type=F32)


def order_of(size):
    order, bit = [0], size // 2
    while bit:
        order += [o ^ bit for o in order]
        bit //= 2
    return order


def swap(x, axis, bit):
    size = lax.axis_size(axis)
    return lax.ppermute(x, axis, [(i, i ^ bit) for i in range(size)])


def after(x, *others):
    return lax.optimization_barrier((x,) + others)[0]


class Course:
    def __init__(self, steps):
        self.steps = steps
        self.result = None
        self.flight = next(steps, None)

    def step(self, x, start=None, behind=None):
        arrived = self.flight
        if arrived is None:
            return x
        arrived = late(arrived, behind)
        x = after(x, arrived)
        try:
            self.flight = self.steps.send((arrived, start))
        except StopIteration as stop:
            self.flight, self.result = None, stop.value
        return x

    def finish(self):
        while self.flight is not None:
            self.step(jnp.zeros((), F32))
        return self.result


def late(x, start):
    return x if start is None else after(x, start)


def gather_steps(x, axis):
    bit = lax.axis_size(axis) // 2
    start, last = None, 1
    while bit > last:
        other, start = yield swap(late(x, start), axis, bit)
        x = jnp.concatenate([x, other], 0)
        bit //= 2
    _, start = yield x
    other, start = yield swap(late(x, start), axis, bit)
    return x, other


def joined(pair):
    return jnp.concatenate(pair, 0)


def sum_steps(keep, send, axis):
    bit, size = 1, lax.axis_size(axis)
    other, start = yield swap(send, axis, bit)
    total = keep + other.astype(F32)
    while bit < size // 2:
        bit *= 2
        half = total.shape[0] // 2
        other, start = yield swap(late(total[half:].astype(LOW), start), axis, bit)
        total = total[:half] + other.astype(F32)
    return total


def sum_all(x, axis):
    bit = 1
    while bit < lax.axis_size(axis):
        x = x + swap(x, axis, bit)
        bit *= 2
    return x


def parts_of(h):
    two = swap(h, "mp", 2)
    one = swap(h, "mp", 1)
    return [h, one, two, swap(two, "mp", 1)]


def parts_sum(even, odd, then=lambda x: x):
    near = then(swap(odd, "mp", 1))
    send = (even[1] + near[1].astype(F32)).astype(LOW)
    return [even, near, swap(send, "mp", 2)], send


def turned_over(v, me):
    size, bit = v.shape[-2], 1
    lead, k = v.shape[:-2], v.shape[-1]
    while bit < size:
        pair = v.reshape(lead + (size // (2 * bit), 2, bit, k))
        flipped = jnp.concatenate([pair[..., 1:, :, :], pair[..., :1, :, :]], -3)
        v = jnp.where((me // bit) % 2 == 1, flipped, pair).reshape(lead + (size, k))
        bit *= 2
    return v


def to_local(v, me, size):
    blocks = turned_over(v.reshape(v.shape[:-1] + (size, v.shape[-1] // size)), me)
    return jnp.concatenate([blocks[..., o, :] for o in order_of(size)], -1)


def from_local(v, me, size):
    blocks = v.reshape(v.shape[:-1] + (size, v.shape[-1] // size))
    order = order_of(size)
    return turned_over(jnp.stack([blocks[..., order.index(k), :] for k in range(size)], -2), me)


def spread(x, axis):
    size = math.prod(lax.axis_size(a) for a in ((axis,) if isinstance(axis, str) else axis))
    copies = jnp.broadcast_to(x[None], (size,) + x.shape)
    return lax.all_to_all(copies, axis, 0, 0, tiled=True)


def exchange(x, axis):
    return lax.all_to_all(x, axis, 0, 0, tiled=True)


def plan():
    betas = jnp.linspace(0.0001, 0.02, 1000, dtype=F32)
    return jnp.cumprod(1.0 - betas)


def pick(table, index):
    grid = jnp.arange(table.shape[0], dtype=jnp.int32)
    return jnp.sum(jnp.where(index[..., None] == grid, table, 0.0), -1)


def normalize(x):
    cent = x - jnp.mean(x, -1, keepdims=True)
    inv = lax.rsqrt(jnp.mean(cent * cent, -1, keepdims=True) + 1e-06)
    return cent * inv, inv


def norm_back(grad, unit, inv, scale):
    d_shift = jnp.sum(grad, 0, keepdims=True)
    d_scale = jnp.sum(grad * unit, 0, keepdims=True)
    g = grad * (1.0 + scale)
    dx = inv * (g - jnp.mean(g, -1, keepdims=True) - unit * jnp.mean(g * unit, -1, keepdims=True))
    return dx, d_shift, d_scale


def place_table(column):
    quarter = D // 4
    omega = 1.0 / 10000.0 ** ((column % quarter).astype(F32) / quarter)
    angle = jnp.arange(SIDE, dtype=F32)[:, None] * omega
    wave = jnp.where((column // quarter) % 2 == 0, jnp.sin(angle), jnp.cos(angle))
    down = column < D // 2
    return jnp.concatenate([jnp.where(down, wave, 0.0), jnp.where(down, 0.0, wave)], 0)


def place_select(single, part, rank):
    local = jnp.arange(part, dtype=jnp.int32)
    full = rank * part + local
    half = SIDE // 2
    down = jnp.where(single, full // SIDE, local // half)
    across = jnp.where(single, full % SIDE, local % half)
    grid = jnp.arange(SIDE, dtype=jnp.int32)
    return jnp.concatenate([down[:, None] == grid, across[:, None] == grid], 1)


def thirds(x):
    high = x.astype(LOW)
    rest = x - high.astype(F32)
    mid = rest.astype(LOW)
    return high, mid, (rest - mid.astype(F32)).astype(LOW)


def time_features(steps):
    half = FREQ // 2
    freqs = jnp.exp(-math.log(10000.0) * jnp.arange(half, dtype=F32) / half)
    angles = steps.astype(F32)[:, None] * freqs
    return jnp.concatenate([jnp.cos(angles), jnp.sin(angles)], -1)


def silu_slope(x):
    s = jax.nn.sigmoid(x)
    return s * (1.0 + x * (1.0 - s))


def call(kernel, name, outs, *args, scalars=0, scratch=(), flops=0, vmem_mb=16):
    smem, vmem = pl.BlockSpec(memory_space=pltpu.SMEM), pl.BlockSpec(memory_space=pltpu.VMEM)
    size = sum(math.prod(o[0]) * jnp.dtype(o[1]).itemsize for o in outs)
    return pl.pallas_call(
        kernel,
        out_shape=[jax.ShapeDtypeStruct(*o) for o in outs],
        in_specs=[smem] * scalars + [vmem] * (len(args) - scalars),
        out_specs=[vmem] * len(outs),
        scratch_shapes=[pltpu.VMEM(*t) for t in scratch],
        compiler_params=pltpu.CompilerParams(vmem_limit_bytes=vmem_mb * 2**20),
        cost_estimate=pl.CostEstimate(flops=1, bytes_accessed=1, transcendentals=0),
        name=name,
    )(*args)


def turned(x):
    return x.astype(F32).T.astype(x.dtype)


def added(even_ref, near_ref, far_ref):
    return even_ref[0] + near_ref[0].astype(F32) + far_ref[...].astype(F32)


def pack_kernel(near_ref, slots_ref, m_mod, m_qkv, m_fc1, m_fc2, m_out, own_ref, other_ref):
    width, hidden = m_out.shape[1], m_fc1.shape[1]

    def put(even, odd):
        at = 0
        for piece in [m_mod[:, k] for k in range(8)] + [m_qkv[k] for k in range(3)] + [slots_ref[...].astype(F32)]:
            even[:, at : at + width] = piece.astype(LOW)
            at += width
        odd[:, :hidden] = m_fc1[...].astype(LOW)
        odd[:, hidden : 2 * hidden] = m_fc2[...].astype(LOW)
        odd[:, 2 * hidden : 2 * hidden + width] = m_out[...].astype(LOW)
        odd[:, 2 * hidden + width :] = jnp.zeros((odd.shape[0], 3 * width), LOW)

    @pl.when(near_ref[0] == 0)
    def _():
        put(own_ref.at[0], other_ref)

    @pl.when(near_ref[0] != 0)
    def _():
        put(other_ref, own_ref.at[0])


def pack(near, slots, m_mod, m_qkv, m_fc1, m_fc2, m_out):
    shape = (m_mod.shape[0], 12 * m_out.shape[1])
    return call(
        pack_kernel,
        "pack",
        [((2,) + shape, LOW), (shape, LOW)],
        *(near, slots, m_mod, m_qkv.transpose(1, 0, 2), m_fc1, m_fc2, m_out),
        scalars=1,
    )


def enter_kernel(x_ref, mods_ref, h_ref):
    unit, _ = normalize(x_ref[...])
    h_ref[...] = (unit * (1.0 + mods_ref[1:2, :]) + mods_ref[0:1, :]).astype(LOW)


def middle_kernel(even_ref, near_ref, far_ref, x_ref, mods_ref, attn_ref, mid_ref, h_ref):
    attn = added(even_ref, near_ref, far_ref)
    attn_ref[...] = attn
    mid = x_ref[...] + mods_ref[2:3, :] * attn
    mid_ref[...] = mid
    unit, _ = normalize(mid)
    h_ref[...] = (unit * (1.0 + mods_ref[4:5, :]) + mods_ref[3:4, :]).astype(LOW)


def final_kernel(
    scale_ref, even_ref, near_ref, far_ref, mid_ref, mods_ref, head_ref, noise_ref,
    out_ref, mlp_ref, head_grad_ref, sums_ref, loss_ref,
):
    mlp = added(even_ref, near_ref, far_ref)
    unit, inv = normalize(mid_ref[...] + mods_ref[5:6, :] * mlp)
    h = (unit * (1.0 + mods_ref[7:8, :]) + mods_ref[6:7, :]).astype(LOW)
    diff = dot(h, head_ref[...], ACROSS) - noise_ref[...]
    loss = jnp.sum(jnp.sum(diff * diff, axis=1, keepdims=True), axis=0, keepdims=True)
    loss_ref[...] = jnp.broadcast_to(scale_ref[0] * loss, loss_ref.shape)
    d_pred = (2.0 * diff * scale_ref[1]).astype(LOW)
    head_grad_ref[...] = dot(d_pred, h, DOWN)
    d_out, d_shift, d_scale = norm_back(dot(d_pred, head_ref[...]), unit, inv, mods_ref[7:8, :])
    out_ref[...] = d_out
    mlp_ref[...] = (d_out * mods_ref[5:6, :]).astype(LOW)
    sums_ref[0:1, :] = jnp.sum(d_out * mlp, 0, keepdims=True)
    sums_ref[1:2, :] = d_shift
    sums_ref[2:3, :] = d_scale


def turn_kernel(
    even_ref, near_ref, far_ref, mid_ref, out_ref, attn_ref, mods_ref, d_mid_ref, d_attn_ref, sums_ref
):
    unit, inv = normalize(mid_ref[...])
    dx, d_shift, d_scale = norm_back(added(even_ref, near_ref, far_ref), unit, inv, mods_ref[4:5, :])
    d_mid = out_ref[...] + dx
    d_mid_ref[...] = d_mid
    d_attn_ref[...] = (d_mid * mods_ref[2:3, :]).astype(LOW)
    sums_ref[0:1, :] = jnp.sum(d_mid * attn_ref[...], 0, keepdims=True)
    sums_ref[1:2, :] = d_shift
    sums_ref[2:3, :] = d_scale


def leave_kernel(
    even_ref, near_ref, far_ref, x_ref, d_mid_ref, mods_ref, noisy_ref, mid_sums_ref, end_sums_ref,
    patch_ref, sums_ref,
):
    unit, inv = normalize(x_ref[...])
    dx, d_shift, d_scale = norm_back(added(even_ref, near_ref, far_ref), unit, inv, mods_ref[1:2, :])
    patch_ref[...] = dot(noisy_ref[...], (d_mid_ref[...] + dx).astype(LOW), DOWN)
    sums_ref[0:1, :] = d_shift
    sums_ref[1:2, :] = d_scale
    sums_ref[2:5, :] = mid_sums_ref[0:3, :]
    sums_ref[5:8, :] = end_sums_ref[0:3, :]


def attend_kernel(
    single_ref, h0_ref, h1_ref, h2_ref, h3_ref, w_ref, o_ref,
    qkv_ref, total_ref, mixed_ref, even_ref, odd_ref, vt_ref,
):
    part = h0_ref.shape[0]
    width = mixed_ref.shape[1]
    for j, ref in enumerate((h0_ref, h1_ref, h2_ref, h3_ref)):
        qkv_ref[j * part : (j + 1) * part, :] = dot(ref[...], w_ref[...]).astype(LOW)
    vt_ref[...] = turned(qkv_ref[:, 2 * width :])

    def run(i, keys):
        mine = pl.ds(pl.multiple_of(i * part, part), part)
        outs = []
        for h in range(width // HEAD_DIM):
            lo = h * HEAD_DIM
            q = qkv_ref[mine, lo : lo + HEAD_DIM] * HEAD_DIM**-0.5
            k = qkv_ref[keys, width + lo : width + lo + HEAD_DIM]
            s = dot(k, q, ACROSS)
            top = jnp.max(s, axis=0, keepdims=True)
            e = jnp.exp(s - top)
            z = jnp.sum(e, axis=0, keepdims=True)
            total_ref[h : h + 1, mine] = top + jnp.log(z)
            outs.append(dot(vt_ref[lo : lo + HEAD_DIM, keys], (e * (1.0 / z)).astype(LOW)))
        mixed_ref[mine, :] = jnp.concatenate(outs, 0).T.astype(LOW)

    def block(i, carry):
        mine = pl.ds(pl.multiple_of(i * part, part), part)

        @pl.when(single_ref[0] == 1)
        def _():
            run(i, slice(None))

        @pl.when(single_ref[0] != 1)
        def _():
            run(i, mine)

        return carry

    lax.fori_loop(0, 4, block, 0)
    for j in range(4):
        term = dot(mixed_ref[j * part : (j + 1) * part, :], o_ref[...], ACROSS)
        if j % 2 == 0:
            even_ref[j // 2] = term
        else:
            odd_ref[j // 2] = term.astype(LOW)


def attend_back_kernel(
    single_ref, qkv_ref, total_ref, d0_ref, d1_ref, d2_ref, d3_ref, w_ref, o_ref,
    grad_ref, even_ref, odd_ref, kt_ref, dk_ref, dv_ref, g_ref,
):
    part = d0_ref.shape[0]
    width = qkv_ref.shape[1] // 3
    heads = width // HEAD_DIM
    for j, ref in enumerate((d0_ref, d1_ref, d2_ref, d3_ref)):
        g_ref[j * part : (j + 1) * part, :] = dot(ref[...], o_ref[...]).astype(LOW)
    kt_ref[...] = turned(qkv_ref[:, width : 2 * width] * HEAD_DIM**-0.5)
    dk_ref[...] = jnp.zeros_like(dk_ref)
    dv_ref[...] = jnp.zeros_like(dv_ref)

    def run(i, keys):
        mine = pl.ds(pl.multiple_of(i * part, part), part)
        outs = []
        for h in range(heads):
            lo = h * HEAD_DIM
            q = qkv_ref[mine, lo : lo + HEAD_DIM] * HEAD_DIM**-0.5
            k = qkv_ref[keys, width + lo : width + lo + HEAD_DIM]
            v = qkv_ref[keys, 2 * width + lo : 2 * width + lo + HEAD_DIM]
            g = g_ref[mine, lo : lo + HEAD_DIM]
            p = jnp.exp(dot(k, q, ACROSS) - total_ref[h : h + 1, mine])
            dp = dot(v, g, ACROSS)
            delta = jnp.sum(dp * p, axis=0, keepdims=True)
            ds = (p * (dp - delta)).astype(LOW)
            dv_ref[h, keys, :] += dot(p.astype(LOW), g)
            dk_ref[h, keys, :] += dot(ds, q)
            outs.append(dot(kt_ref[lo : lo + HEAD_DIM, keys], ds))
        grad_ref[mine, :width] = jnp.concatenate(outs, 0).T.astype(LOW)

    def block(i, carry):
        @pl.when(single_ref[0] == 1)
        def _():
            run(i, slice(None))

        @pl.when(single_ref[0] != 1)
        def _():
            run(i, pl.ds(pl.multiple_of(i * part, part), part))

        return carry

    lax.fori_loop(0, 4, block, 0)
    for h in range(heads):
        lo = h * HEAD_DIM
        grad_ref[:, width + lo : width + lo + HEAD_DIM] = dk_ref[h].astype(LOW)
        grad_ref[:, 2 * width + lo : 2 * width + lo + HEAD_DIM] = dv_ref[h].astype(LOW)
    for j in range(4):
        term = dot(grad_ref[j * part : (j + 1) * part, :], w_ref[...], ACROSS)
        if j % 2 == 0:
            even_ref[j // 2] = term
        else:
            odd_ref[j // 2] = term.astype(LOW)


def halves(keep_ref, send_ref, columns, value):
    half = keep_ref.shape[0]
    keep_ref[:, columns] = value[:half]
    send_ref[:, columns] = value[half:].astype(LOW)


def attend_grads_kernel(h0, h1, h2, h3, grad_ref, d0, d1, d2, d3, mixed_ref, keep_ref, send_ref):
    part, width = h0.shape[0], mixed_ref.shape[1]
    rows = lambda j: slice(j * part, (j + 1) * part)
    halves(
        keep_ref, send_ref, slice(0, 3 * width),
        sum(dot(h[...], grad_ref[rows(j), :], DOWN) for j, h in enumerate((h0, h1, h2, h3))),
    )
    halves(
        keep_ref, send_ref, slice(3 * width, 4 * width),
        sum(dot(d[...], mixed_ref[rows(j), :], DOWN) for j, d in enumerate((d0, d1, d2, d3))),
    )


def feed_kernel(h0, h1, h2, h3, w_ref, act_ref, slope_ref, even_ref, odd_ref):
    part, hidden = h0.shape[0], act_ref.shape[1]
    for j, h in enumerate((h0, h1, h2, h3)):
        rows = slice(j * part, (j + 1) * part)
        upper = dot(h[...], w_ref[:, :hidden])
        gate = 0.5 * (1.0 + lax.erf(upper * 0.5**0.5))
        act = (upper * gate).astype(LOW)
        act_ref[rows, :] = act
        slope = gate + upper * jnp.exp(-0.5 * upper * upper) * (2.0 * math.pi) ** -0.5
        slope_ref[rows, :] = slope.astype(LOW)
        term = dot(act, w_ref[:, hidden:], ACROSS)
        if j % 2 == 0:
            even_ref[j // 2] = term
        else:
            odd_ref[j // 2] = term.astype(LOW)


def feed_back_kernel(d0, d1, d2, d3, slope_ref, w_ref, upper_ref, even_ref, odd_ref):
    part, hidden = d0.shape[0], slope_ref.shape[1]
    for j, d in enumerate((d0, d1, d2, d3)):
        rows = slice(j * part, (j + 1) * part)
        d_upper = (dot(d[...], w_ref[:, hidden:]) * slope_ref[rows, :].astype(F32)).astype(LOW)
        upper_ref[rows, :] = d_upper
        term = dot(d_upper, w_ref[:, :hidden], ACROSS)
        if j % 2 == 0:
            even_ref[j // 2] = term
        else:
            odd_ref[j // 2] = term.astype(LOW)


def feed_grads_kernel(h0, h1, h2, h3, x_ref, keep_ref, send_ref):
    part = h0.shape[0]
    value = sum(
        dot(h[...], x_ref[j * part : (j + 1) * part, :], DOWN) for j, h in enumerate((h0, h1, h2, h3))
    )
    halves(keep_ref, send_ref, slice(None), value)


def muon_kernel(columns, span, order_ref, coef_ref, plan_ref, mom_ref, *refs):
    grads, (out_ref, x_ref, b_ref, e_ref, r_ref, turn_ref) = refs[:-6], refs[-6:]
    third = NS_COEF[2]
    size, width = x_ref.shape
    count, pairs = mom_ref.shape[2], mom_ref.shape[0]
    coef = coef_ref[0]
    spans = [slice(i, min(i + size, width)) for i in range(0, width, size)]

    tall = size < count * 2 * pairs
    squares = jnp.zeros((1, 1), F32)
    for place in range(2 * pairs):
        true = order_ref[place]
        if len(grads) == 1:
            grad = grads[0][true, :, slice(*span)].astype(F32)
        elif len(grads[0].shape) == 4:
            grad = dot(grads[0][lax.shift_right_logical(true, 1), place // pairs], grads[1][...])
        else:
            grad = grads[place // pairs][place % pairs].astype(F32)
        mom = mom_ref[lax.shift_right_logical(true, 1), place // pairs, :, slice(*columns)]
        x = MU * mom.astype(F32) + coef * grad
        if tall:
            turn_ref[place * count : (place + 1) * count, :] = x
        else:
            x_ref[place * count : (place + 1) * count, :] = x
        squares = squares + jnp.sum(jnp.sum(x * x, axis=0, keepdims=True), axis=1, keepdims=True)
    inv = 1.0 / (jnp.sqrt(squares) + 1e-07)
    x_ref[...] = (turn_ref[...].T if tall else x_ref[...]) * inv
    b_ref[...] = x_ref[...].astype(LOW)

    def gram(shift):
        e = sum(dot(b_ref[:, span], b_ref[:, span], ACROSS) for span in spans)
        row = lax.broadcasted_iota(jnp.int32, e.shape, 0)
        column = lax.broadcasted_iota(jnp.int32, e.shape, 1)
        e = e - jnp.where(row == column, shift, 0.0)
        e_ref[...] = e
        r_ref[...] = e.astype(LOW)

    def turn(i, carry):
        centre, slope = plan_ref[i, 0], plan_ref[i, 1]
        gram(plan_ref[i, 2])
        r_ref[...] = (slope * e_ref[...] + third * dot(r_ref[...], r_ref[...])).astype(LOW)
        for span in spans:
            x = centre * x_ref[:, span] + dot(r_ref[...], b_ref[:, span])
            x_ref[:, span] = x
            b_ref[:, span] = x.astype(LOW)
        return carry

    last = len(NS_SHIFT) - 1
    lax.fori_loop(0, last, turn, 0)
    gram(plan_ref[last, 2])
    both = [slice(0, count), slice(pairs * count, (pairs + 1) * count)]
    scaled = 0.2 * math.sqrt(max(size, width))
    if tall:
        poly = plan_ref[last, 1] * e_ref[...] + third * dot(r_ref[...], r_ref[...])
        x = jnp.concatenate([x_ref[:, own].T for own in both], 0)
        x = scaled * (plan_ref[last, 0] * x + dot(x.astype(LOW), poly.astype(LOW)))
        out_ref[0] = x[:count].astype(LOW)
        out_ref[1] = x[count:].astype(LOW)
        return
    e = jnp.concatenate([e_ref[own, :] for own in both], 0)
    poly = (plan_ref[last, 1] * e + third * dot(e.astype(LOW), r_ref[...])).astype(LOW)
    for span in spans:
        x = jnp.concatenate([x_ref[own, span] for own in both], 0)
        x = scaled * (plan_ref[last, 0] * x + dot(poly, b_ref[:, span]))
        out_ref[0, :, span] = x[:count].astype(LOW)
        out_ref[1, :, span] = x[count:].astype(LOW)


def muon_rows(order, coef, old, block, columns, grads, span=None):
    pairs, _, count, _ = old.shape
    deep, width = 2 * pairs * count, columns[1] - columns[0]
    size, long = (width, deep) if 2 * width <= deep else (deep, width)
    first, second, third = NS_COEF
    plan = [[first + second * s + third * s * s, second + 2.0 * third * s, s] for s in NS_SHIFT]
    smem, vmem = pl.BlockSpec(memory_space=pltpu.SMEM), pl.BlockSpec(memory_space=pltpu.VMEM)
    return pl.pallas_call(
        functools.partial(muon_kernel, columns, span),
        grid=(1,),
        out_shape=jax.ShapeDtypeStruct((2, count, width), LOW),
        in_specs=[smem, smem, smem, pl.BlockSpec((pairs, 2, count, block[0]), lambda i: (0, 0, 0, block[1]))]
        + [vmem] * len(grads),
        out_specs=vmem,
        scratch_shapes=[
            pltpu.VMEM((size, long), F32),
            pltpu.VMEM((size, long), LOW),
            pltpu.VMEM((size, size), F32),
            pltpu.VMEM((size, size), LOW),
            pltpu.VMEM((deep, width) if size < deep else (8, 128), F32),
        ],
        compiler_params=pltpu.CompilerParams(vmem_limit_bytes=32 * 2**20),
        cost_estimate=pl.CostEstimate(flops=1, bytes_accessed=1, transcendentals=0),
        name="muon",
    )(order, coef, jnp.array(plan, F32), old, *grads)


def finish_kernel(
    near_ref, coef_ref, own_a, got_a, own_b, got_b, g_at, g_fc1, g_fc2, g_mod,
    w_qkv, w_out, w_fc1, w_fc2, w_mod, m_qkv, m_out, m_fc1, m_fc2, m_mod,
    n_qkv, n_out, n_fc1, n_fc2, n_mod, k_qkv, k_out, k_fc1, k_fc2, k_mod,
):
    width, hidden = w_out.shape[1], w_fc1.shape[1]
    coef = coef_ref[0]
    mine = near_ref[0] == 0

    def put(place, weight, mom, new, kept, update, grad):
        new[place] = weight[place] * (1.0 - LR_MUON * DECAY) - LR_MUON * update
        kept[place] = MU * mom[place] + coef * grad

    a, b = own_a[...].astype(F32), got_a[...].astype(F32)
    u_mod, u_fc = jnp.where(mine, a, b), jnp.where(mine, b, a)
    a, b = own_b[...].astype(F32), got_b[...].astype(F32)
    u_qkv, u_out = jnp.where(mine, a, b), jnp.where(mine, b, a)[:, :width]
    for k in range(3):
        span = slice(k * width, (k + 1) * width)
        put(k, w_qkv, m_qkv, n_qkv, k_qkv, u_qkv[:, span], g_at[:, span])
    for k in range(8):
        span = slice(k * width, (k + 1) * width)
        put((slice(None), k), w_mod, m_mod, n_mod, k_mod, u_mod[:, span], g_mod[:, span])
    put(slice(None), w_out, m_out, n_out, k_out, u_out, g_at[:, 3 * width :])
    put(slice(None), w_fc2, m_fc2, n_fc2, k_fc2, u_fc[:, :hidden], g_fc2[...])
    put(slice(None), w_fc1, m_fc1, n_fc1, k_fc1, u_fc[:, hidden:], g_fc1[...])


def finish(near, coef, flats, weights, moms):
    rows = flats[0].shape[0]
    step = rows // 2 if rows % 32 == 0 else rows
    smem = pl.BlockSpec(memory_space=pltpu.SMEM)

    def block(a):
        if a.ndim == 2:
            return pl.BlockSpec((step, a.shape[1]), lambda i: (i, 0))
        if a.shape[0] == rows:
            return pl.BlockSpec((step,) + a.shape[1:], lambda i: (i, 0, 0))
        return pl.BlockSpec((a.shape[0], step, a.shape[2]), lambda i: (0, i, 0))

    first = lambda a: a.transpose(1, 0, 2)
    arrays = [first(weights[0]), *weights[1:], first(moms[0]), *moms[1:]]
    outs = pl.pallas_call(
        finish_kernel,
        grid=(rows // step,),
        out_shape=[jax.ShapeDtypeStruct(a.shape, F32) for a in arrays],
        in_specs=[smem, smem] + [block(a) for a in (*flats, *arrays)],
        out_specs=[block(a) for a in arrays],
        compiler_params=pltpu.CompilerParams(vmem_limit_bytes=32 * 2**20),
        name="finish",
    )(near, coef, *flats, *arrays)
    return [first(outs[0]), *outs[1:5]], [first(outs[5]), *outs[6:]]


def body(
    latents,
    noise,
    segment_ids,
    timesteps,
    labels,
    w_qkv,
    w_out,
    w_fc1,
    w_fc2,
    w_mod,
    w_head,
    w_cond,
    mom_qkv,
    mom_out,
    mom_fc1,
    mom_fc2,
    mom_mod,
    first_head,
    second_head,
    first_cond,
    second_cond,
):
    n_dp, n_mp = lax.axis_size("dp"), lax.axis_size("mp")
    me, rank = lax.axis_index("dp"), lax.axis_index("mp")
    near = me % 2
    tokens = latents.shape[0]
    part = tokens // n_mp
    rows = w_qkv.shape[0]
    width = w_qkv.shape[2]
    hidden = w_fc1.shape[1]
    half = D // 2
    place = [me ^ o for o in order_of(n_dp)]
    places = me ^ jnp.array(order_of(n_dp), jnp.int32)

    single = jnp.max(segment_ids) == 0
    time1_own = w_cond[:, PIN : PIN + FREQ].astype(LOW)
    digits = [v for a in (timesteps, labels) for v in (a.reshape(-1) // SIDE, a.reshape(-1) % SIDE)]
    note = jnp.concatenate(digits + [single.astype(jnp.int32)[None]]).astype(LOW)
    note = jnp.pad(note, (0, FREQ - note.shape[0]))
    thin = jnp.concatenate([w_cond[:, :PIN].astype(LOW), w_head.astype(LOW)], 1).reshape(-1, FREQ)
    thin_rows = thin.shape[0]
    fill = -(rows + thin_rows) % 16 or 16
    packet = spread(jnp.concatenate([time1_own, thin, jnp.broadcast_to(note, (fill, FREQ))], 0), "dp")
    packet = packet.reshape(n_dp, rows + thin_rows + fill, FREQ)

    time1_b = packet[:, :rows].reshape(D, FREQ)
    thin = packet[:, rows : rows + thin_rows].reshape(n_dp, rows, 2 * PIN).astype(F32)
    thin = jnp.concatenate([lax.dynamic_index_in_dim(thin, p, 0) for p in place], 0)
    thin = thin.reshape(D, 2 * PIN).T.astype(LOW)
    patch_b, head_b = thin[:PIN], thin[PIN:]
    notes = packet[:, rows + thin_rows].astype(jnp.int32)
    steps = notes[:, :SLOTS] * SIDE + notes[:, SLOTS : 2 * SLOTS]
    kinds = (notes[:, 2 * SLOTS : 3 * SLOTS] * SIDE + notes[:, 3 * SLOTS : 4 * SLOTS]).reshape(-1)
    singles = notes[:, 4 * SLOTS] == 1

    time2_b = w_cond[:, PIN + FREQ : PIN + FREQ + D].astype(LOW)
    table_b = w_cond[:, PIN + FREQ + D :].astype(LOW)
    mod_b = jnp.concatenate([w_mod[:, k].astype(LOW) for k in range(8)], 1)
    feat_b = time_features(steps.reshape(-1)).astype(LOW)
    slots_all = feat_b.shape[0]
    silu_t_b = jax.nn.silu(dot(feat_b, time1_b, ACROSS)).astype(LOW)
    onehot = (kinds[:, None] == jnp.arange(CLASSES, dtype=jnp.int32)).astype(LOW)
    qkv_own = jnp.concatenate([w_qkv[:, k].astype(LOW) for k in range(3)] + [w_out.astype(LOW)], 1)
    proj_way = Course(gather_steps(after(qkv_own, silu_t_b), "dp"))
    cond = dot(silu_t_b, time2_b, ACROSS) + dot(onehot, table_b, ACROSS)
    silu_c_b = jax.nn.silu(cond).astype(LOW)
    mod_part = exchange(dot(silu_c_b, mod_b).reshape(n_dp, SLOTS, -1), "dp")
    mod_cols = jnp.sum(mod_part, 0).reshape(SLOTS, 8, width)
    mod_cols = proj_way.step(mod_cols, mod_cols)
    slots_own = jnp.pad(silu_c_b.T, ((0, 0), (0, width - slots_all)))
    own_pack, other_pack = pack(near[None], slots_own, mom_mod, mom_qkv, mom_fc1, mom_fc2, mom_out)
    other_pack = swap(other_pack, "dp", 1)
    part_slots = segment_ids[::part]
    outgoing = jnp.sum(
        jnp.where((part_slots[:, None] == jnp.arange(SLOTS))[:, :, None, None], mod_cols[None], 0.0), 1
    )
    mods = exchange(outgoing, "mp").transpose(1, 0, 2).reshape(8, n_mp * width)
    mods = after(to_local(mods, me, n_dp), other_pack)
    slot = jnp.sum(jnp.where(jnp.arange(n_mp) == rank, part_slots, 0))

    abar = pick(plan(), steps)
    snr = abar / (1.0 - abar)
    slot_weight = jnp.minimum(snr, GAMMA) / snr
    weight_total = part * jnp.sum(jnp.where(singles[:, None], n_mp * slot_weight[:, :1] / SLOTS, slot_weight))
    mine = (jnp.arange(n_dp)[:, None] == me) & (jnp.arange(SLOTS) == slot)
    my_slot = lambda a: jnp.sum(jnp.where(mine, a, 0.0))
    abar_tok, weight_tok = my_slot(abar), my_slot(slot_weight)
    lat = lax.dynamic_slice_in_dim(latents, rank * part, part, 0)
    noi = lax.dynamic_slice_in_dim(noise, rank * part, part, 0)
    noisy_b = (jnp.sqrt(abar_tok) * lat + jnp.sqrt(1.0 - abar_tok) * noi).astype(LOW)
    picks = place_select(single, part, rank).astype(LOW)
    left = jnp.concatenate([noisy_b, picks, picks, picks], 1)
    column = (after(places, silu_t_b)[:, None] * rows + jnp.arange(rows, dtype=jnp.int32)).reshape(-1)
    x_in = dot(left, jnp.concatenate([patch_b, *thirds(place_table(column))], 0))
    alone = single.astype(jnp.int32)[None]

    tile = ((part, D), F32)
    tile_b = ((part, D), LOW)
    terms = [((2, part, D), F32), ((2, part, D), LOW)]
    sums = ((8, D), F32)
    thin_grad = ((PIN, D), F32)
    shares = [((half, D), F32), ((half, D), LOW)]
    (h_in,) = call(enter_kernel, "enter", [tile_b], x_in, mods)
    h_in = proj_way.step(h_in)
    feed_own = jnp.concatenate([w_fc1, w_fc2], 1).astype(LOW)
    feed_way = Course(gather_steps(after(feed_own, h_in), "dp"))
    h_in = parts_of(h_in)
    h_in[1] = proj_way.step(h_in[1])
    h_in[3] = feed_way.step(h_in[3])
    proj = joined(proj_way.finish())
    qkv_b, out_b = proj[:, : 3 * width], proj[:, 3 * width :]
    qkv, totals, mixed_b, *attn_terms = call(
        attend_kernel,
        "attend",
        [((tokens, 3 * width), LOW), ((8, tokens), F32), ((tokens, width), LOW), *terms],
        *(alone, *h_in, qkv_b, out_b),
        scalars=1,
        scratch=[((width, tokens), LOW)],
        flops=8 * tokens * tokens * width + 8 * tokens * D * width,
    )
    attn_terms, sent = parts_sum(*attn_terms, lambda near: feed_way.step(feed_way.step(near)))
    sides = [[side + 2 * i for i in range(n_dp // 2)] for side in range(2)]
    old = after(lax.dynamic_update_slice(own_pack, other_pack[None], (1, 0, 0)), sent)
    old = lax.all_gather(old, "dp", axis=0, axis_index_groups=sides)
    attn, x_mid, h_mid = call(middle_kernel, "middle", [tile, tile, tile_b], *attn_terms, x_in, mods)
    h_mid = parts_of(h_mid)
    feed_b = joined(feed_way.finish())

    act_b, slope, *mlp_terms = call(
        feed_kernel,
        "feed",
        [((tokens, hidden), LOW), ((tokens, hidden), LOW), *terms],
        *(*h_mid, feed_b),
        flops=4 * tokens * D * hidden,
    )
    scales = jnp.stack([weight_tok, weight_tok / weight_total])
    mlp_terms, _ = parts_sum(*mlp_terms)
    d_out, d_mlp, d_head, end_sums, loss_part = call(
        final_kernel,
        "final",
        [tile, tile_b, thin_grad, sums, ((1, 128), F32)],
        *(scales, *mlp_terms, x_mid, mods, head_b, noi),
        scalars=1,
    )

    d_mlp = parts_of(d_mlp)
    d_mlp[3] = after(d_mlp[3], old)
    flops = 2 * tokens * D * hidden
    d_upper, *terms_mid = call(
        feed_back_kernel,
        "feed_back",
        [((tokens, hidden), LOW), *terms],
        *(*d_mlp, slope, feed_b),
        flops=2 * flops,
    )
    terms_mid, sent = parts_sum(*terms_mid)
    act_late, d_upper = lax.optimization_barrier((act_b, d_upper, sent))[:2]
    fc2_terms = call(feed_grads_kernel, "feed_grads", shares, *d_mlp, act_late, flops=flops)
    fc2_way = Course(sum_steps(*fc2_terms, "dp"))
    fc1_terms = call(feed_grads_kernel, "feed_grads", shares, *h_mid, d_upper, flops=flops)
    fc1_way = Course(sum_steps(*fc1_terms, "dp"))
    d_mid, d_attn, mid_sums = call(
        turn_kernel, "turn", [tile, tile_b, sums], *terms_mid, x_mid, d_out, attn, mods
    )
    d_attn = parts_of(d_attn)
    d_attn[1] = fc2_way.step(d_attn[1])
    d_attn[3] = fc1_way.step(fc2_way.step(d_attn[3]))
    d_qkv, even, odd = call(
        attend_back_kernel,
        "attend_back",
        [((tokens, 3 * width), LOW), *terms],
        *(alone, qkv, totals, *d_attn, qkv_b, out_b),
        scalars=1,
        scratch=[((width, tokens), LOW)]
        + [((width // HEAD_DIM, tokens, HEAD_DIM), F32)] * 2
        + [((tokens, width), LOW)],
        flops=20 * tokens * tokens * width + 8 * tokens * D * width,
    )
    odd = fc1_way.step(fc2_way.step(odd))
    sum_fc2 = fc2_way.finish()
    fc2_way = Course(gather_steps(sum_fc2.astype(LOW), "dp"))
    terms_in, sent = parts_sum(even, odd)
    at_terms = call(
        attend_grads_kernel,
        "attend_grads",
        shares,
        *(*h_in, after(d_qkv, sent), *d_attn, mixed_b),
        flops=8 * tokens * D * width,
    )
    at_way = Course(sum_steps(*at_terms, "dp"))
    terms_in[2] = fc2_way.step(fc1_way.step(terms_in[2], behind=at_terms[1]), behind=at_terms[1])
    sum_fc1 = fc1_way.finish()
    fc1_way = Course(gather_steps(sum_fc1.astype(LOW), "dp"))
    d_patch, d_mods = call(
        leave_kernel, "leave", [thin_grad, sums], *terms_in, x_in, d_mid, mods, noisy_b, mid_sums, end_sums
    )

    d_mods = from_local(d_mods, me, n_dp).reshape(8, n_mp, width).transpose(1, 0, 2)
    blocks = jnp.broadcast_to(d_mods[None], (n_dp,) + d_mods.shape).reshape((n_dp * n_mp,) + d_mods.shape[1:])
    blocks = exchange(blocks, ("dp", "mp")).reshape(n_dp, n_mp, 8, width)
    blocks = at_way.step(blocks, blocks)
    first_only = (jnp.arange(SLOTS) == 0)[:, None, None]
    d_mod_all = jnp.where(
        singles[:, None, None, None], jnp.where(first_only, jnp.sum(blocks, 1, keepdims=True), 0.0), blocks
    )
    d_mod_all = d_mod_all.astype(LOW).reshape(slots_all, 8 * width)
    g_mod = dot(silu_c_b, d_mod_all, DOWN)
    d_cond_part = dot(d_mod_all, mod_b, ACROSS) * silu_slope(cond)
    d_silu_t_part = lax.dot_general(d_cond_part, time2_b.astype(F32), ALONG, precision=HIGH)
    thick = jnp.concatenate(
        [d_silu_t_part.reshape(-1, n_dp, rows), from_local(jnp.concatenate([d_patch, d_head], 0), me, n_dp)], 0
    )
    thick = jnp.sum(exchange(thick.transpose(1, 0, 2), "dp"), 0)
    for way in (at_way, fc1_way, fc2_way, fc2_way):
        thick = way.step(thick, thick)
    thick = sum_all(jnp.concatenate([thick, d_cond_part], 0), "mp")
    hidden_t = dot(feat_b, time1_own, ACROSS)
    d_hidden = thick[:slots_all] * silu_slope(hidden_t)
    g_patch = thick[slots_all : slots_all + PIN]
    g_head = thick[slots_all + PIN : slots_all + 2 * PIN].T
    d_cond = thick[slots_all + 2 * PIN :]
    right = jnp.concatenate(
        [
            jnp.concatenate([jnp.zeros((slots_all, PIN), LOW), feat_b, jnp.zeros((slots_all, D + CLASSES), LOW)], 1),
            jnp.eye(PIN, PIN + FREQ + D + CLASSES, dtype=LOW),
            jnp.concatenate([jnp.zeros((slots_all, PIN + FREQ), LOW), silu_t_b, onehot], 1),
        ],
        0,
    )
    g_cond = dot(
        jnp.concatenate(thirds(jnp.concatenate([d_hidden, g_patch, d_cond], 0)), 0),
        jnp.concatenate([right] * 3, 0),
        DOWN,
    )

    square = lambda g: jnp.sum(g * g)
    sum_at = at_way.finish()
    split_sq = square(sum_fc1) + square(sum_fc2) + square(sum_at) + square(g_mod)
    tally = jnp.stack([split_sq + (square(g_head) + square(g_cond)) / n_mp, loss_part[0, 0]])
    tally = jnp.sum(spread(jnp.broadcast_to(tally[:, None], (2, 128)), ("dp", "mp")), 0)
    tally = fc1_way.step(fc1_way.step(fc2_way.step(tally)), tally)
    grad_norm = jnp.sqrt(tally[0, 0])
    loss_sum = tally[1, 0]
    coef = jnp.minimum(1.0, CLIP / (grad_norm + 1e-06))

    halves_of = lambda way: [g.reshape(n_dp // 2, rows, -1) for g in way.finish()]
    all_fc2 = halves_of(fc2_way)
    all_fc1 = halves_of(fc1_way)
    factor = coef[None]
    all_at = jnp.broadcast_to(sum_at.astype(LOW)[None], (n_dp,) + sum_at.shape)
    all_at = exchange(after(all_at, factor), "dp")
    span = 8 * width

    silu_c_all = old[:, :, :, 11 * width : 11 * width + slots_all]

    def one_mod():
        return muon_rows(places, factor, old, (span, 0), (0, span), (silu_c_all, d_mod_all))

    def one_fc2():
        mine = muon_rows(places, factor, old, (hidden, 1), (0, hidden), all_fc2)
        return jnp.pad(mine, ((0, 0), (0, 0), (0, span - hidden)))

    def one_fc1():
        mine = muon_rows(places, factor, old, (hidden, 0), (0, hidden), all_fc1)
        return jnp.concatenate([both[:, :, :hidden], mine], 2)

    at_block = (4 * width, 2)

    def one_qkv():
        return muon_rows(places, factor, old, at_block, (0, 3 * width), (all_at,), (0, 3 * width))

    def one_out():
        mine = muon_rows(places, factor, old, at_block, (0, width), (all_at,), (3 * width, 4 * width))
        return jnp.pad(mine, ((0, 0), (0, 0), (0, 2 * width)))

    both = lax.cond(near == 0, one_mod, one_fc2)
    both = lax.cond(near == 0, lambda: both, one_fc1)
    last = lax.cond(near == 0, one_qkv, one_out)
    both = after(both, last)
    new_weights, new_moms = finish(
        near[None],
        factor,
        (both[0], swap(both[1], "dp", 1), last[0], swap(last[1], "dp", 1), sum_at, sum_fc1, sum_fc2, g_mod),
        (w_qkv, w_out, w_fc1, w_fc2, w_mod),
        (mom_qkv, mom_out, mom_fc1, mom_fc2, mom_mod),
    )
    coef = after(coef, last)

    adam_out = []
    for master, first, second, grad in (
        (w_head, first_head, second_head, g_head),
        (w_cond, first_cond, second_cond, g_cond),
    ):
        clipped = coef * grad
        first = BETA_ONE * first + (1.0 - BETA_ONE) * clipped
        second = BETA_TWO * second + (1.0 - BETA_TWO) * clipped * clipped
        update = first / (1.0 - BETA_ONE**STEP) / (jnp.sqrt(second / (1.0 - BETA_TWO**STEP)) + EPS_ADAM)
        adam_out.append((master - LR_ADAM * (update + DECAY * master), first, second))
    return (
        *new_weights,
        adam_out[0][0],
        adam_out[1][0],
        *new_moms,
        adam_out[0][1],
        adam_out[0][2],
        adam_out[1][1],
        adam_out[1][2],
        loss_sum,
        weight_total,
        grad_norm,
    )


def solution(mesh):
    row, wide, cube = P("dp", None), P("dp", "mp"), P("dp", None, "mp")
    in_specs = (
        *(row, row, P("dp"), row, row),
        *(cube, wide, wide, wide, cube, row, row),
        *(cube, wide, wide, wide, cube),
        *(row, row, row, row),
    )
    out_specs = (
        *(cube, wide, wide, wide, cube, row, row),
        *(cube, wide, wide, wide, cube),
        *(row, row, row, row),
        *(P(), P(), P()),
    )
    return jax.shard_map(body, mesh=mesh, in_specs=in_specs, out_specs=out_specs, check_vma=False)
```

profile of v0, /device:TPU:0, one launch (start us, length us, event | category | flops | bytes accessed | tf_op | source)
XLA Modules:
  0.0 411.3 jit_solution(13741674668711276448)
XLA Ops:
  11.7 7.3 %all-to-all-start = ((bf16[8,112,256]{2,1,0:T(8,128)(2,1)}), bf16[8,112,256]{2,1,0:T(8,128)(2,1)S(1)}, u32[]{:S(2)}, u32[]{:S(2)}) async-start(bf16[8,112,256]{2,1,0:T(8,128)(2,1)} %broadcast_in_dim.178), calls=%async_computation | async-start | bytes 917504 | tf_op jit(solution)/shard_map/all_to_all | solution.py:161
  24.6 7.5 %all-to-all-done = bf16[8,112,256]{2,1,0:T(8,128)(2,1)S(1)} async-done(((bf16[8,112,256]{2,1,0:T(8,128)(2,1)}), bf16[8,112,256]{2,1,0:T(8,128)(2,1)S(1)}, u32[]{:S(2)}, u32[]{:S(2)}) %all-to-all-start) | async-done | bytes 458784 | tf_op jit(solution)/shard_map/all_to_all | solution.py:161
  62.3 6.3 %collective-permute-done.2 = bf16[192,768]{1,0:T(8,128)(2,1)S(1)} collective-permute-done((bf16[192,768]{1,0:T(8,128)(2,1)S(1)}, bf16[192,768]{1,0:T(8,128)(2,1)S(1)}, u32[]{:S(2)}, u32[]{:S(2)}) %collective-permute-start.2) | collective-permute-done | bytes 294944 | tf_op jit(solution)/shard_map/ppermute | solution.py:53
  72.3 7.0 %collective-permute-done.4.h2_ref.h2 = bf16[256,768]{1,0:T(8,128)(2,1)S(1)} collective-permute-done((bf16[256,768]{1,0:T(8,128)(2,1)S(1)}, bf16[256,768]{1,0:T(8,128)(2,1)S(1)}, u32[]{:S(2)}, u32[]{:S(2)}) %collective-permute-start.4) | collective-permute-done | bytes 393248 | tf_op jit(solution)/shard_map/ppermute | solution.py:53
  79.3 7.1 %collective-permute-done.6 = bf16[96,1536]{1,0:T(8,128)(2,1)S(1)} collective-permute-done((bf16[96,1536]{1,0:T(8,128)(2,1)S(1)}, bf16[96,1536]{1,0:T(8,128)(2,1)S(1)}, u32[]{:S(2)}, u32[]{:S(2)}) %collective-permute-start.6) | collective-permute-done | bytes 294944 | tf_op jit(solution)/shard_map/ppermute | solution.py:53
  88.1 8.4 %attend.1 = (bf16[1024,576]{1,0:T(8,128)(2,1)S(1)}, f32[8,1024]{1,0:T(8,128)S(1)}, bf16[1024,192]{1,0:T(8,128)(2,1)S(1)}, f32[2,256,768]{2,1,0:T(8,128)S(1)}, bf16[2,256,768]{2,1,0:T(8,128)(2,1)}) custom-call(s32[1]{0:T(128)} %bitcast.5.single_ref, bf16[256,768]{1,0:T(8,128)(2,1)S(1)} %enter.1.h0_ref.h0, ...), custom_call_target="tpu_custom_call" | custom-call | flops 1 | bytes 1 | tf_op jit(solution)/shard_map/attend/pallas_call | solution.py:233
  109.4 10.4 %collective-permute-done.10.far_ref = bf16[256,768]{1,0:T(8,128)(2,1)S(1)} collective-permute-done((bf16[256,768]{1,0:T(8,128)(2,1)}, bf16[256,768]{1,0:T(8,128)(2,1)S(1)}, u32[]{:S(2)}, u32[]{:S(2)}) %collective-permute-start.10) | collective-permute-done | bytes 393248 | tf_op jit(solution)/shard_map/ppermute | solution.py:53
  124.9 9.4 %collective-permute-done.12.h2 = bf16[256,768]{1,0:T(8,128)(2,1)S(1)} collective-permute-done((bf16[256,768]{1,0:T(8,128)(2,1)S(1)}, bf16[256,768]{1,0:T(8,128)(2,1)S(1)}, u32[]{:S(2)}, u32[]{:S(2)}) %collective-permute-start.12) | collective-permute-done | bytes 393248 | tf_op jit(solution)/shard_map/ppermute | solution.py:53
  148.6 8.8 %collective-permute-done.16.far_ref = bf16[256,768]{1,0:T(8,128)(2,1)} collective-permute-done((bf16[256,768]{1,0:T(8,128)(2,1)}, bf16[256,768]{1,0:T(8,128)(2,1)}, u32[]{:S(2)}, u32[]{:S(2)}) %collective-permute-start.16) | collective-permute-done | bytes 393248 | tf_op jit(solution)/shard_map/ppermute | solution.py:53
  166.9 9.9 %collective-permute-done.18.d2.h2 = bf16[256,768]{1,0:T(8,128)(2,1)S(1)} collective-permute-done((bf16[256,768]{1,0:T(8,128)(2,1)}, bf16[256,768]{1,0:T(8,128)(2,1)S(1)}, u32[]{:S(2)}, u32[]{:S(2)}) %collective-permute-start.18) | collective-permute-done | bytes 393248 | tf_op jit(solution)/shard_map/ppermute | solution.py:53
  205.0 7.5 %collective-permute-done.24.far_ref = bf16[256,768]{1,0:T(8,128)(2,1)S(1)} collective-permute-done((bf16[256,768]{1,0:T(8,128)(2,1)S(1)}, bf16[256,768]{1,0:T(8,128)(2,1)S(1)}, u32[]{:S(2)}, u32[]{:S(2)}) %collective-permute-start.24) | collective-permute-done | bytes 393248 | tf_op jit(solution)/shard_map/ppermute | solution.py:53
  216.2 6.5 %collective-permute-start.29 = (bf16[192,768]{1,0:T(8,128)(2,1)S(1)}, bf16[192,768]{1,0:T(8,128)(2,1)S(1)}, u32[]{:S(2)}, u32[]{:S(2)}) collective-permute-start(bf16[192,768]{1,0:T(8,128)(2,1)S(1)} %slice.623), channel_id=1, source_target_pairs={{0,8},{4,12},{8,0},{12,4},{16,24},{20,28},{24,16},{28,20},{1,9},{5... | collective-permute-start | bytes 884744 | tf_op jit(solution)/shard_map/ppermute | solution.py:53
  222.7 5.4 %collective-permute-done.21 = bf16[384,768]{1,0:T(8,128)(2,1)S(1)} collective-permute-done((bf16[384,768]{1,0:T(8,128)(2,1)S(1)}, bf16[384,768]{1,0:T(8,128)(2,1)S(1)}, u32[]{:S(2)}, u32[]{:S(2)}) %collective-permute-start.21) | collective-permute-done | bytes 589856 | tf_op jit(solution)/shard_map/ppermute | solution.py:53
  228.2 6.3 %collective-permute-start.22 = (bf16[192,768]{1,0:T(8,128)(2,1)S(1)}, bf16[192,768]{1,0:T(8,128)(2,1)S(1)}, u32[]{:S(2)}, u32[]{:S(2)}) collective-permute-start(bf16[192,768]{1,0:T(8,128)(2,1)S(1)} %slice.624), channel_id=1, source_target_pairs={{0,8},{4,12},{8,0},{12,4},{16,24},{20,28},{24,16},{28,20},{1,9},{5... | collective-permute-start | bytes 884744 | tf_op jit(solution)/shard_map/ppermute | solution.py:53
  236.3 7.0 %attend_back.1 = (bf16[1024,576]{1,0:T(8,128)(2,1)S(1)}, f32[2,256,768]{2,1,0:T(8,128)S(1)}, bf16[2,256,768]{2,1,0:T(8,128)(2,1)S(1)}) custom-call(s32[1]{0:T(128)} %bitcast.5.single_ref, bf16[1024,576]{1,0:T(8,128)(2,1)S(1)} %copy-done.52, f32[8,1024]{1,0:T(8,128)S(1)} %get-tuple-element.236.total_ref, bf16[256,768]{1,0:T(8,128)(2,1)S(1)} %get-tuple-element.239.d0_ref.d0, ...), custom_call_target="tpu_custom_call" | custom-call | flops 1 | bytes 1 | tf_op jit(solution)/shard_map/attend_back/pallas_call | solution.py:233
  245.3 6.3 %collective-permute-start.23 = (bf16[96,768]{1,0:T(8,128)(2,1)S(1)}, bf16[96,768]{1,0:T(8,128)(2,1)S(1)}, u32[]{:S(2)}, u32[]{:S(2)}) collective-permute-start(bf16[96,768]{1,0:T(8,128)(2,1)S(1)} %slice.627), channel_id=1, source_target_pairs={{0,16},{4,20},{8,24},{12,28},{16,0},{20,4},{24,8},{28,12},{1,17},{... | collective-permute-start | bytes 442376 | tf_op jit(solution)/shard_map/ppermute | solution.py:53
  258.5 6.3 %collective-permute-done.34 = bf16[96,768]{1,0:T(8,128)(2,1)S(1)} collective-permute-done((bf16[96,768]{1,0:T(8,128)(2,1)S(1)}, bf16[96,768]{1,0:T(8,128)(2,1)S(1)}, u32[]{:S(2)}, u32[]{:S(2)}) %collective-permute-start.34) | collective-permute-done | bytes 147488 | tf_op jit(solution)/shard_map/ppermute | solution.py:53
  276.8 7.1 %all-to-all-done.3 = f32[32,8,192]{2,1,0:T(8,128)S(1)} async-done(((f32[32,8,192]{2,1,0:T(8,128)}), f32[32,8,192]{2,1,0:T(8,128)S(1)}, u32[]{:S(2)}, u32[]{:S(2)}) %all-to-all-start.3) | async-done | bytes 196640 | tf_op jit(solution)/shard_map/all_to_all | solution.py:165
  316.1 9.7 %all_to_all.35 = f32[32,2,128]{2,1,0:T(2,128)S(1)} all-to-all(f32[32,2,128]{2,1,0:T(2,128)S(1)} %broadcast_in_dim_broadcast_in_dim_broadcast_in_dim.2), channel_id=1, replica_groups=mesh['dp'=8,'mp'=4] {'dp','mp'}, dimensions={0} | all-to-all | bytes 65536 | tf_op jit(solution)/shard_map/all_to_all | solution.py:161
  335.7 28.0 %conditional.3 = (bf16[2,96,1536]{2,1,0:T(8,128)(2,1)S(1)}) conditional(s32[]{:T(128)} %convert_element_type.312, (s32[8]{0:T(128)S(1)}, f32[1]{0:T(128)}, f32[5,3]{1,0:T(8,128)S(1)}, bf16[4,2,96,2304]{3,2,1,0:T(8,128)(2,1)}, bf16[384,768]{1,0:T(8,128)(2,1)S(1)}, /*index=5*/bf16[384,768]{1,0:T(8,128)(2,1)}) %tuple.216, (s32[8]{0:T(128)S(1)}, ...), branch_computations={%region_19.20_spmd, %region_20.21_spmd} | conditional | flops 1 | bytes 884747 | solution.py:930
  336.7 26.8 %muon.6 = bf16[2,96,1536]{2,1,0:T(8,128)(2,1)S(1)} custom-call(s32[8]{0:T(128)S(1)} %get-tuple-element.76.order_ref, f32[1]{0:T(128)} %get-tuple-element.77.coef_ref, f32[5,3]{1,0:T(8,128)S(1)} %get-tuple-element.78.plan_ref, bf16[4,2,96,2304]{3,2,1,0:T(8,128)(2,1)} %get-tuple-element.294, bf16[4,2,96,32]{3,2,1,0:T(8,128)(2,1)S(1)} %slice.449.refs_0_, ...), custom_call_target="tpu_custom_call" | custom-call | flops 1 | bytes 1 | tf_op jit(solution)/shard_map/cond/branch_1_fun/muon/pallas_call | solution.py:580
  363.8 16.3 %conditional.5 = (bf16[2,96,576]{2,1,0:T(8,128)(2,1)S(1)}) conditional(s32[]{:T(128)} %convert_element_type.312, (s32[8]{0:T(128)S(1)}, f32[1]{0:T(128)}, f32[5,3]{1,0:T(8,128)S(1)}, bf16[4,2,96,2304]{3,2,1,0:T(8,128)(2,1)}, bf16[8,96,768]{2,1,0:T(8,128)(2,1)S(1)}) %tuple.219, (s32[8]{0:T(128)S(1)}, f32[1]{0:T(128)}, f32[5,3]{1,0:T(8,128)S(1)}, ...), branch_computations={%region_23.24_spmd, %region_24.25_spmd} | conditional | flops 1 | bytes 294923 | solution.py:932
  363.8 16.1 %muon.9 = bf16[2,96,576]{2,1,0:T(8,128)(2,1)S(1)} custom-call(s32[8]{0:T(128)S(1)} %get-tuple-element.94.order_ref, f32[1]{0:T(128)} %get-tuple-element.95.coef_ref, f32[5,3]{1,0:T(8,128)S(1)} %get-tuple-element.96.plan_ref, bf16[4,2,96,2304]{3,2,1,0:T(8,128)(2,1)} %get-tuple-element.97.mom_ref, bf16[8,96,768]{2,1,0:T(8,128)(2,1)S(1)} %get-tuple-element.98.refs_0_), custom_call_target="tpu_custom_call" | custom-call | flops 1 | bytes 1 | tf_op jit(solution)/shard_map/cond/branch_1_fun/muon/pallas_call | solution.py:580
  380.2 8.4 %collective-permute-start.44 = (bf16[96,1536]{1,0:T(8,128)(2,1)S(1)}, bf16[96,1536]{1,0:T(8,128)(2,1)S(1)}, u32[]{:S(2)}, u32[]{:S(2)}) collective-permute-start(bf16[96,1536]{1,0:T(8,128)(2,1)S(1)} %get-tuple-element.445), channel_id=1, source_target_pairs={{0,4},{4,0},{8,12},{12,8},{16,20},{20,16},{24,28},{28,24},{1,5},{5... | collective-permute-start | bytes 884744 | tf_op jit(solution)/shard_map/ppermute | solution.py:53
  (621 shorter events, 188.2 us)
Async XLA Ops:
  11.7 20.4 %all-to-all-start = ((bf16[8,112,256]{2,1,0:T(8,128)(2,1)}), bf16[8,112,256]{2,1,0:T(8,128)(2,1)S(1)}, u32[]{:S(2)}, u32[]{:S(2)}) async-start(bf16[8,112,256]{2,1,0:T(8,128)(2,1)} %broadcast_in_dim.178), calls=%async_computation | async-start | bytes 917504 | tf_op jit(solution)/shard_map/all_to_all | solution.py:161
  47.3 14.7 %collective-permute-start.1 = (bf16[96,2304]{1,0:T(8,128)(2,1)S(1)}, bf16[96,2304]{1,0:T(8,128)(2,1)S(1)}, u32[]{:S(2)}, u32[]{:S(2)}) collective-permute-start(bf16[96,2304]{1,0:T(8,128)(2,1)S(1)} %get-tuple-element.208), channel_id=1, source_target_pairs={{0,4},{4,0},{8,12},{12,8},{16,20},{20,16},{24,28},{28,24},{1,5},{5... | collective-permute-start | bytes 1327112 | tf_op jit(solution)/shard_map/ppermute | solution.py:53
  57.3 123.9 %all-gather.3.cloned.1.call-start = ((), (), s32[]{:S(2)}) async-start(), calls=%async_computation.7 | async-start | bytes 4423680 | tf_op jit(solution)/shard_map/all_gather | solution.py:778
  71.1 16.2 %collective-permute-start.7 = (bf16[384,768]{1,0:T(8,128)(2,1)}, bf16[384,768]{1,0:T(8,128)(2,1)S(1)}, u32[]{:S(2)}, u32[]{:S(2)}) collective-permute-start(bf16[384,768]{1,0:T(8,128)(2,1)} %get-tuple-element.462), channel_id=1, source_target_pairs={{0,4},{4,0},{8,12},{12,8},{16,20},{20,16},{24,28},{28,24},{1,5},{5... | collective-permute-start | bytes 1769480 | tf_op jit(solution)/shard_map/ppermute | solution.py:53
  71.1 15.2 %collective-permute-start.6 = (bf16[96,1536]{1,0:T(8,128)(2,1)S(1)}, bf16[96,1536]{1,0:T(8,128)(2,1)S(1)}, u32[]{:S(2)}, u32[]{:S(2)}) collective-permute-start(bf16[96,1536]{1,0:T(8,128)(2,1)S(1)} %pad_maximum_fusion.5), channel_id=1, source_target_pairs={{0,16},{4,20},{8,24},{12,28},{16,0},{20,4},{24,8},{28,12},{1,17},{... | collective-permute-start | bytes 884744 | tf_op jit(solution)/shard_map/ppermute | solution.py:53
  72.3 15.0 %collective-permute-start.3 = (bf16[256,768]{1,0:T(8,128)(2,1)S(1)}, bf16[256,768]{1,0:T(8,128)(2,1)S(1)}, u32[]{:S(2)}, u32[]{:S(2)}) collective-permute-start(bf16[256,768]{1,0:T(8,128)(2,1)S(1)} %enter.1.h0_ref.h0), channel_id=1, source_target_pairs={{0,1},{1,0},{2,3},{3,2},{4,5},{5,4},{6,7},{7,6},{8,9},{9,8},{10,11... | collective-permute-start | bytes 1179656 | tf_op jit(solution)/shard_map/ppermute | solution.py:53
  87.3 15.1 %collective-permute-start.9 = (bf16[192,1536]{1,0:T(8,128)(2,1)}, bf16[192,1536]{1,0:T(8,128)(2,1)}, u32[]{:S(2)}, u32[]{:S(2)}) collective-permute-start(bf16[192,1536]{1,0:T(8,128)(2,1)} %pad_maximum_fusion.1), channel_id=1, source_target_pairs={{0,8},{4,12},{8,0},{12,4},{16,24},{20,28},{24,16},{28,20},{1,9},{5... | collective-permute-start | bytes 1769480 | tf_op jit(solution)/shard_map/ppermute | solution.py:53
  106.6 28.7 %collective-permute-start.14 = (bf16[384,1536]{1,0:T(8,128)(2,1)}, bf16[384,1536]{1,0:T(8,128)(2,1)S(1)}, u32[]{:S(2)}, u32[]{:S(2)}) collective-permute-start(bf16[384,1536]{1,0:T(8,128)(2,1)} %copy-done.112), channel_id=1, source_target_pairs={{0,4},{4,0},{8,12},{12,8},{16,20},{20,16},{24,28},{28,24},{1,5},{5... | collective-permute-start | bytes 3538952 | tf_op jit(solution)/shard_map/ppermute | solution.py:53
  199.6 16.4 %collective-permute-start.26 = (bf16[384,768]{1,0:T(8,128)(2,1)S(1)}, bf16[384,768]{1,0:T(8,128)(2,1)S(1)}, u32[]{:S(2)}, u32[]{:S(2)}) collective-permute-start(bf16[384,768]{1,0:T(8,128)(2,1)S(1)} %get-tuple-element.241), channel_id=1, source_target_pairs={{0,4},{4,0},{8,12},{12,8},{16,20},{20,16},{24,28},{28,24},{1,5},{5... | collective-permute-start | bytes 1769480 | tf_op jit(solution)/shard_map/ppermute | solution.py:53
  204.4 23.6 %collective-permute-start.21 = (bf16[384,768]{1,0:T(8,128)(2,1)S(1)}, bf16[384,768]{1,0:T(8,128)(2,1)S(1)}, u32[]{:S(2)}, u32[]{:S(2)}) collective-permute-start(bf16[384,768]{1,0:T(8,128)(2,1)S(1)} %get-tuple-element.234), channel_id=1, source_target_pairs={{0,4},{4,0},{8,12},{12,8},{16,20},{20,16},{24,28},{28,24},{1,5},{5... | collective-permute-start | bytes 1769480 | tf_op jit(solution)/shard_map/ppermute | solution.py:53
  214.4 20.3 %collective-permute-start.25 = (bf16[256,768]{1,0:T(8,128)(2,1)S(1)}, bf16[256,768]{1,0:T(8,128)(2,1)S(1)}, u32[]{:S(2)}, u32[]{:S(2)}) collective-permute-start(bf16[256,768]{1,0:T(8,128)(2,1)S(1)} %get-tuple-element.239.d0_ref.d0), channel_id=1, source_target_pairs={{0,1},{1,0},{2,3},{3,2},{4,5},{5,4},{6,7},{7,6},{8,9},{9,8},{10,11... | collective-permute-start | bytes 1179656 | tf_op jit(solution)/shard_map/ppermute | solution.py:53
  214.5 20.1 %collective-permute-start.27 = (bf16[256,768]{1,0:T(8,128)(2,1)S(1)}, bf16[256,768]{1,0:T(8,128)(2,1)S(1)}, u32[]{:S(2)}, u32[]{:S(2)}) collective-permute-start(bf16[256,768]{1,0:T(8,128)(2,1)S(1)} %get-tuple-element.239.d0_ref.d0), channel_id=1, source_target_pairs={{0,2},{1,3},{2,0},{3,1},{4,6},{5,7},{6,4},{7,5},{8,10},{9,11},{10,... | collective-permute-start | bytes 1179656 | tf_op jit(solution)/shard_map/ppermute | solution.py:53
  216.2 18.4 %collective-permute-start.29 = (bf16[192,768]{1,0:T(8,128)(2,1)S(1)}, bf16[192,768]{1,0:T(8,128)(2,1)S(1)}, u32[]{:S(2)}, u32[]{:S(2)}) collective-permute-start(bf16[192,768]{1,0:T(8,128)(2,1)S(1)} %slice.623), channel_id=1, source_target_pairs={{0,8},{4,12},{8,0},{12,4},{16,24},{20,28},{24,16},{28,20},{1,9},{5... | collective-permute-start | bytes 884744 | tf_op jit(solution)/shard_map/ppermute | solution.py:53
  228.2 16.9 %collective-permute-start.22 = (bf16[192,768]{1,0:T(8,128)(2,1)S(1)}, bf16[192,768]{1,0:T(8,128)(2,1)S(1)}, u32[]{:S(2)}, u32[]{:S(2)}) collective-permute-start(bf16[192,768]{1,0:T(8,128)(2,1)S(1)} %slice.624), channel_id=1, source_target_pairs={{0,8},{4,12},{8,0},{12,4},{16,24},{20,28},{24,16},{28,20},{1,9},{5... | collective-permute-start | bytes 884744 | tf_op jit(solution)/shard_map/ppermute | solution.py:53
  256.6 17.3 %collective-permute-start.32 = (bf16[384,768]{1,0:T(8,128)(2,1)}, bf16[384,768]{1,0:T(8,128)(2,1)}, u32[]{:S(2)}, u32[]{:S(2)}) collective-permute-start(bf16[384,768]{1,0:T(8,128)(2,1)} %get-tuple-element.253), channel_id=1, source_target_pairs={{0,4},{4,0},{8,12},{12,8},{16,20},{20,16},{24,28},{28,24},{1,5},{5... | collective-permute-start | bytes 1769480 | tf_op jit(solution)/shard_map/ppermute | solution.py:53
  264.9 28.0 %collective-permute-start.37 = (bf16[96,768]{1,0:T(8,128)(2,1)S(1)}, bf16[96,768]{1,0:T(8,128)(2,1)S(1)}, u32[]{:S(2)}, u32[]{:S(2)}) collective-permute-start(bf16[96,768]{1,0:T(8,128)(2,1)S(1)} %get-tuple-element.439), channel_id=1, source_target_pairs={{0,16},{4,20},{8,24},{12,28},{16,0},{20,4},{24,8},{28,12},{1,17},{... | collective-permute-start | bytes 442376 | tf_op jit(solution)/shard_map/ppermute | solution.py:53
  265.7 28.0 %collective-permute-start.38 = (bf16[192,768]{1,0:T(8,128)(2,1)}, bf16[192,768]{1,0:T(8,128)(2,1)}, u32[]{:S(2)}, u32[]{:S(2)}) collective-permute-start(bf16[192,768]{1,0:T(8,128)(2,1)} %pad_maximum_fusion.6), channel_id=1, source_target_pairs={{0,8},{4,12},{8,0},{12,4},{16,24},{20,28},{24,16},{28,20},{1,9},{5... | collective-permute-start | bytes 884744 | tf_op jit(solution)/shard_map/ppermute | solution.py:53
  268.1 15.9 %all-to-all-start.3 = ((f32[32,8,192]{2,1,0:T(8,128)}), f32[32,8,192]{2,1,0:T(8,128)S(1)}, u32[]{:S(2)}, u32[]{:S(2)}) async-start(f32[32,8,192]{2,1,0:T(8,128)} %bitcast.61), calls=%async_computation.3 | async-start | bytes 524288 | tf_op jit(solution)/shard_map/all_to_all | solution.py:165
  283.9 15.5 %collective-permute-start.35 = (bf16[192,768]{1,0:T(8,128)(2,1)}, bf16[192,768]{1,0:T(8,128)(2,1)}, u32[]{:S(2)}, u32[]{:S(2)}) collective-permute-start(bf16[192,768]{1,0:T(8,128)(2,1)} %slice.622), channel_id=1, source_target_pairs={{0,8},{4,12},{8,0},{12,4},{16,24},{20,28},{24,16},{28,20},{1,9},{5... | collective-permute-start | bytes 884744 | tf_op jit(solution)/shard_map/ppermute | solution.py:53
  304.0 23.7 %collective-permute-start.41 = (bf16[384,768]{1,0:T(8,128)(2,1)S(1)}, bf16[384,768]{1,0:T(8,128)(2,1)S(1)}, u32[]{:S(2)}, u32[]{:S(2)}) collective-permute-start(bf16[384,768]{1,0:T(8,128)(2,1)S(1)} %pad_maximum_fusion.2), channel_id=1, source_target_pairs={{0,4},{4,0},{8,12},{12,8},{16,20},{20,16},{24,28},{28,24},{1,5},{5... | collective-permute-start | bytes 1769480 | tf_op jit(solution)/shard_map/ppermute | solution.py:53
  304.5 21.3 %collective-permute-start.42 = (bf16[192,768]{1,0:T(8,128)(2,1)}, bf16[192,768]{1,0:T(8,128)(2,1)}, u32[]{:S(2)}, u32[]{:S(2)}) collective-permute-start(bf16[192,768]{1,0:T(8,128)(2,1)} %pad_maximum_fusion.7), channel_id=1, source_target_pairs={{0,8},{4,12},{8,0},{12,4},{16,24},{20,28},{24,16},{28,20},{1,9},{5... | collective-permute-start | bytes 884744 | tf_op jit(solution)/shard_map/ppermute | solution.py:53
  330.1 33.7 %all-to-all-start.6 = ((bf16[8,96,768]{2,1,0:T(8,128)(2,1)}), bf16[8,96,768]{2,1,0:T(8,128)(2,1)S(1)}, u32[]{:S(2)}, u32[]{:S(2)}) async-start(bf16[8,96,768]{2,1,0:T(8,128)(2,1)} %broadcast_in_dim.202), calls=%async_computation.6 | async-start | bytes 2359296 | tf_op jit(solution)/shard_map/all_to_all | solution.py:165
  333.8 30.0 %collective-permute-start.43 = (bf16[384,768]{1,0:T(8,128)(2,1)}, bf16[384,768]{1,0:T(8,128)(2,1)}, u32[]{:S(2)}, u32[]{:S(2)}) collective-permute-start(bf16[384,768]{1,0:T(8,128)(2,1)} %pad_maximum_fusion.3), channel_id=1, source_target_pairs={{0,4},{4,0},{8,12},{12,8},{16,20},{20,16},{24,28},{28,24},{1,5},{5... | collective-permute-start | bytes 1769480 | tf_op jit(solution)/shard_map/ppermute | solution.py:53
  380.2 17.5 %collective-permute-start.44 = (bf16[96,1536]{1,0:T(8,128)(2,1)S(1)}, bf16[96,1536]{1,0:T(8,128)(2,1)S(1)}, u32[]{:S(2)}, u32[]{:S(2)}) collective-permute-start(bf16[96,1536]{1,0:T(8,128)(2,1)S(1)} %get-tuple-element.445), channel_id=1, source_target_pairs={{0,4},{4,0},{8,12},{12,8},{16,20},{20,16},{24,28},{28,24},{1,5},{5... | collective-permute-start | bytes 884744 | tf_op jit(solution)/shard_map/ppermute | solution.py:53
  (164 other events, 1131.3 us)
Sparse Core Ops, SparseCore 0:
  106.7 74.5 all-gather.2
where the time goes:
time: 419 us; the launch traced here: 411 us
  waiting for transfers between devices  119 us (28%)
  Pallas kernels  85.7 us (20%)
  starting transfers between devices  80.7 us (19%)
  local copies, waits for them, and re-layouts  51.9 us (12%)
  other arithmetic  30.5 us (7%)
  between operations  27.1 us (6%)
  blocking collectives  9.67 us (2%)
  matrix products  6.36 us (2%)
    ppermute x46, waiting for transfers between devices, swap(): return lax.ppermute(x, axis, [(i, i ^ bit) for i in range(size)])  94 us
    ppermute x46, starting transfers between devices, swap(): return lax.ppermute(x, axis, [(i, i ^ bit) for i in range(size)])  52.8 us
    pallas_call x2, Pallas kernels, muon_rows(): pl.pallas_call(functools.partial(muon_kernel, columns, span), grid=(1,),...  42.9 us
    pallas_call x13, Pallas kernels, call(): pl.pallas_call(kernel, out_shape=[jax.ShapeDtypeStruct(*o) for o in outs]...  38.7 us
    unnamed x307, local copies, waits for them, and re-layouts  37.3 us
    all_to_all x5, starting transfers between devices, exchange(): return lax.all_to_all(x, axis, 0, 0, tiled=True)  20.3 us
    all_to_all x5, waiting for transfers between devices, exchange(): return lax.all_to_all(x, axis, 0, 0, tiled=True)  15.5 us
    all_to_all x1, blocking collectives, spread(): return lax.all_to_all(copies, axis, 0, 0, tiled=True)  9.67 us
  transfers between devices with their start and end apart: 53, of which 25 were waited for; matrix products, arithmetic and copies ran while one was open for 12% of the time, Pallas kernels for 14%

commit v1 on v0

--- a/solution.py
+++ b/solution.py
@@ -68,7 +68,7 @@
         if arrived is None:
             return x
         arrived = late(arrived, behind)
-        x = after(x, arrived)
+        x = after(x, *arrived) if isinstance(arrived, tuple) else after(x, arrived)
         try:
             self.flight = self.steps.send((arrived, start))
         except StopIteration as stop:
@@ -82,7 +82,9 @@
 
 
 def late(x, start):
-    return x if start is None else after(x, start)
+    if start is None:
+        return x
+    return lax.optimization_barrier((*x, start))[:-1] if isinstance(x, tuple) else after(x, start)
 
 
 def gather_steps(x, axis):
@@ -95,6 +97,18 @@
     _, start = yield x
     other, start = yield swap(late(x, start), axis, bit)
     return x, other
+
+
+def quarter_steps(x, axis):
+    bit, start = lax.axis_size(axis) // 2, None
+    while bit > 2:
+        other, start = yield swap(late(x, start), axis, bit)
+        x = jnp.concatenate([x, other], 0)
+        bit //= 2
+    x = late(x, start)
+    (second, third), start = yield swap(x, axis, 2), swap(x, axis, 1)
+    fourth, start = yield swap(late(second, start), axis, 1)
+    return [x, second, third, fourth]
 
 
 def joined(pair):
@@ -516,10 +530,11 @@
         true = order_ref[place]
         if len(grads) == 1:
             grad = grads[0][true, :, slice(*span)].astype(F32)
-        elif len(grads[0].shape) == 4:
+        elif len(grads) == 2:
             grad = dot(grads[0][lax.shift_right_logical(true, 1), place // pairs], grads[1][...])
         else:
-            grad = grads[place // pairs][place % pairs].astype(F32)
+            quarter, row = divmod(place * count, grads[0].shape[0])
+            grad = grads[quarter][row : row + count, :].astype(F32)
         mom = mom_ref[lax.shift_right_logical(true, 1), place // pairs, :, slice(*columns)]
         x = MU * mom.astype(F32) + coef * grad
         if tall:
@@ -597,38 +612,45 @@
     )(order, coef, jnp.array(plan, F32), old, *grads)
 
 
-def finish_kernel(
-    near_ref, coef_ref, own_a, got_a, own_b, got_b, g_at, g_fc1, g_fc2, g_mod,
-    w_qkv, w_out, w_fc1, w_fc2, w_mod, m_qkv, m_out, m_fc1, m_fc2, m_mod,
-    n_qkv, n_out, n_fc1, n_fc2, n_mod, k_qkv, k_out, k_fc1, k_fc2, k_mod,
-):
+def weights_kernel(near_ref, own_a, got_a, own_b, got_b, w_qkv, w_out, w_fc1, w_fc2, w_mod, n_qkv, n_out, n_fc1, n_fc2, n_mod):
     width, hidden = w_out.shape[1], w_fc1.shape[1]
-    coef = coef_ref[0]
     mine = near_ref[0] == 0
 
-    def put(place, weight, mom, new, kept, update, grad):
+    def put(place, weight, new, update):
         new[place] = weight[place] * (1.0 - LR_MUON * DECAY) - LR_MUON * update
-        kept[place] = MU * mom[place] + coef * grad
 
     a, b = own_a[...].astype(F32), got_a[...].astype(F32)
     u_mod, u_fc = jnp.where(mine, a, b), jnp.where(mine, b, a)
     a, b = own_b[...].astype(F32), got_b[...].astype(F32)
     u_qkv, u_out = jnp.where(mine, a, b), jnp.where(mine, b, a)[:, :width]
     for k in range(3):
-        span = slice(k * width, (k + 1) * width)
-        put(k, w_qkv, m_qkv, n_qkv, k_qkv, u_qkv[:, span], g_at[:, span])
+        put(k, w_qkv, n_qkv, u_qkv[:, k * width : (k + 1) * width])
     for k in range(8):
-        span = slice(k * width, (k + 1) * width)
-        put((slice(None), k), w_mod, m_mod, n_mod, k_mod, u_mod[:, span], g_mod[:, span])
-    put(slice(None), w_out, m_out, n_out, k_out, u_out, g_at[:, 3 * width :])
-    put(slice(None), w_fc2, m_fc2, n_fc2, k_fc2, u_fc[:, :hidden], g_fc2[...])
-    put(slice(None), w_fc1, m_fc1, n_fc1, k_fc1, u_fc[:, hidden:], g_fc1[...])
-
-
-def finish(near, coef, flats, weights, moms):
+        put((slice(None), k), w_mod, n_mod, u_mod[:, k * width : (k + 1) * width])
+    put(slice(None), w_out, n_out, u_out)
+    put(slice(None), w_fc2, n_fc2, u_fc[:, :hidden])
+    put(slice(None), w_fc1, n_fc1, u_fc[:, hidden:])
+
+
+def momenta_kernel(coef_ref, g_at, g_fc1, g_fc2, g_mod, m_qkv, m_out, m_fc1, m_fc2, m_mod, k_qkv, k_out, k_fc1, k_fc2, k_mod):
+    width = m_out.shape[1]
+    coef = coef_ref[0]
+
+    def put(place, mom, kept, grad):
+        kept[place] = MU * mom[place] + coef * grad
+
+    for k in range(3):
+        put(k, m_qkv, k_qkv, g_at[:, k * width : (k + 1) * width])
+    for k in range(8):
+        put((slice(None), k), m_mod, k_mod, g_mod[:, k * width : (k + 1) * width])
+    put(slice(None), m_out, k_out, g_at[:, 3 * width :])
+    put(slice(None), m_fc2, k_fc2, g_fc2[...])
+    put(slice(None), m_fc1, k_fc1, g_fc1[...])
+
+
+def by_rows(kernel, name, scalar, flats, arrays):
     rows = flats[0].shape[0]
     step = rows // 2 if rows % 32 == 0 else rows
-    smem = pl.BlockSpec(memory_space=pltpu.SMEM)
 
     def block(a):
         if a.ndim == 2:
@@ -637,18 +659,17 @@
             return pl.BlockSpec((step,) + a.shape[1:], lambda i: (i, 0, 0))
         return pl.BlockSpec((a.shape[0], step, a.shape[2]), lambda i: (0, i, 0))
 
-    first = lambda a: a.transpose(1, 0, 2)
-    arrays = [first(weights[0]), *weights[1:], first(moms[0]), *moms[1:]]
+    arrays = [arrays[0].transpose(1, 0, 2), *arrays[1:]]
     outs = pl.pallas_call(
-        finish_kernel,
+        kernel,
         grid=(rows // step,),
         out_shape=[jax.ShapeDtypeStruct(a.shape, F32) for a in arrays],
-        in_specs=[smem, smem] + [block(a) for a in (*flats, *arrays)],
+        in_specs=[pl.BlockSpec(memory_space=pltpu.SMEM)] + [block(a) for a in (*flats, *arrays)],
         out_specs=[block(a) for a in arrays],
         compiler_params=pltpu.CompilerParams(vmem_limit_bytes=32 * 2**20),
-        name="finish",
-    )(near, coef, *flats, *arrays)
-    return [first(outs[0]), *outs[1:5]], [first(outs[5]), *outs[6:]]
+        name=name,
+    )(scalar, *flats, *arrays)
+    return [outs[0].transpose(1, 0, 2), *outs[1:]]
 
 
 def body(
@@ -729,7 +750,6 @@
         jnp.where((part_slots[:, None] == jnp.arange(SLOTS))[:, :, None, None], mod_cols[None], 0.0), 1
     )
     mods = exchange(outgoing, "mp").transpose(1, 0, 2).reshape(8, n_mp * width)
-    mods = after(to_local(mods, me, n_dp), other_pack)
     slot = jnp.sum(jnp.where(jnp.arange(n_mp) == rank, part_slots, 0))
 
     abar = pick(plan(), steps)
@@ -739,6 +759,17 @@
     mine = (jnp.arange(n_dp)[:, None] == me) & (jnp.arange(SLOTS) == slot)
     my_slot = lambda a: jnp.sum(jnp.where(mine, a, 0.0))
     abar_tok, weight_tok = my_slot(abar), my_slot(slot_weight)
+    right = jnp.concatenate(
+        [
+            jnp.concatenate([jnp.zeros((slots_all, PIN), LOW), feat_b, jnp.zeros((slots_all, D + CLASSES), LOW)], 1),
+            jnp.eye(PIN, PIN + FREQ + D + CLASSES, dtype=LOW),
+            jnp.concatenate([jnp.zeros((slots_all, PIN + FREQ), LOW), silu_t_b, onehot], 1),
+        ],
+        0,
+    )
+    right = jnp.concatenate([right] * 3, 0)
+    scales = jnp.stack([weight_tok, weight_tok / weight_total])
+    mods = after(to_local(mods, me, n_dp), other_pack, right, scales)
     lat = lax.dynamic_slice_in_dim(latents, rank * part, part, 0)
     noi = lax.dynamic_slice_in_dim(noise, rank * part, part, 0)
     noisy_b = (jnp.sqrt(abar_tok) * lat + jnp.sqrt(1.0 - abar_tok) * noi).astype(LOW)
@@ -758,6 +789,9 @@
     h_in = proj_way.step(h_in)
     feed_own = jnp.concatenate([w_fc1, w_fc2], 1).astype(LOW)
     feed_way = Course(gather_steps(after(feed_own, h_in), "dp"))
+    sides = [[side + 2 * i for i in range(n_dp // 2)] for side in range(2)]
+    stacked = lax.dynamic_update_slice(own_pack, other_pack[None], (1, 0, 0))
+    old = lax.all_gather(after(stacked, h_in), "dp", axis=0, axis_index_groups=sides)
     h_in = parts_of(h_in)
     h_in[1] = proj_way.step(h_in[1])
     h_in[3] = feed_way.step(h_in[3])
@@ -772,10 +806,7 @@
         scratch=[((width, tokens), LOW)],
         flops=8 * tokens * tokens * width + 8 * tokens * D * width,
     )
-    attn_terms, sent = parts_sum(*attn_terms, lambda near: feed_way.step(feed_way.step(near)))
-    sides = [[side + 2 * i for i in range(n_dp // 2)] for side in range(2)]
-    old = after(lax.dynamic_update_slice(own_pack, other_pack[None], (1, 0, 0)), sent)
-    old = lax.all_gather(old, "dp", axis=0, axis_index_groups=sides)
+    attn_terms, _ = parts_sum(*attn_terms, lambda near: feed_way.step(feed_way.step(near)))
     attn, x_mid, h_mid = call(middle_kernel, "middle", [tile, tile, tile_b], *attn_terms, x_in, mods)
     h_mid = parts_of(h_mid)
     feed_b = joined(feed_way.finish())
@@ -787,7 +818,6 @@
         *(*h_mid, feed_b),
         flops=4 * tokens * D * hidden,
     )
-    scales = jnp.stack([weight_tok, weight_tok / weight_total])
     mlp_terms, _ = parts_sum(*mlp_terms)
     d_out, d_mlp, d_head, end_sums, loss_part = call(
         final_kernel,
@@ -798,7 +828,6 @@
     )
 
     d_mlp = parts_of(d_mlp)
-    d_mlp[3] = after(d_mlp[3], old)
     flops = 2 * tokens * D * hidden
     d_upper, *terms_mid = call(
         feed_back_kernel,
@@ -816,7 +845,7 @@
     d_mid, d_attn, mid_sums = call(
         turn_kernel, "turn", [tile, tile_b, sums], *terms_mid, x_mid, d_out, attn, mods
     )
-    d_attn = parts_of(d_attn)
+    d_attn = parts_of(after(d_attn, old))
     d_attn[1] = fc2_way.step(d_attn[1])
     d_attn[3] = fc1_way.step(fc2_way.step(d_attn[3]))
     d_qkv, even, odd = call(
@@ -832,7 +861,7 @@
     )
     odd = fc1_way.step(fc2_way.step(odd))
     sum_fc2 = fc2_way.finish()
-    fc2_way = Course(gather_steps(sum_fc2.astype(LOW), "dp"))
+    fc2_way = Course(quarter_steps(sum_fc2.astype(LOW), "dp"))
     terms_in, sent = parts_sum(even, odd)
     at_terms = call(
         attend_grads_kernel,
@@ -844,7 +873,7 @@
     at_way = Course(sum_steps(*at_terms, "dp"))
     terms_in[2] = fc2_way.step(fc1_way.step(terms_in[2], behind=at_terms[1]), behind=at_terms[1])
     sum_fc1 = fc1_way.finish()
-    fc1_way = Course(gather_steps(sum_fc1.astype(LOW), "dp"))
+    fc1_way = Course(quarter_steps(sum_fc1.astype(LOW), "dp"))
     d_patch, d_mods = call(
         leave_kernel, "leave", [thin_grad, sums], *terms_in, x_in, d_mid, mods, noisy_b, mid_sums, end_sums
     )
@@ -865,42 +894,37 @@
         [d_silu_t_part.reshape(-1, n_dp, rows), from_local(jnp.concatenate([d_patch, d_head], 0), me, n_dp)], 0
     )
     thick = jnp.sum(exchange(thick.transpose(1, 0, 2), "dp"), 0)
-    for way in (at_way, fc1_way, fc2_way, fc2_way):
-        thick = way.step(thick, thick)
-    thick = sum_all(jnp.concatenate([thick, d_cond_part], 0), "mp")
+    thick = jnp.concatenate([thick, d_cond_part], 0)
+    chip = thick + swap(thick, "mp", 1)
+    for way in (at_way, fc1_way, fc2_way):
+        chip = way.step(chip, thick)
+    thick = chip + swap(chip, "mp", 2)
     hidden_t = dot(feat_b, time1_own, ACROSS)
     d_hidden = thick[:slots_all] * silu_slope(hidden_t)
     g_patch = thick[slots_all : slots_all + PIN]
     g_head = thick[slots_all + PIN : slots_all + 2 * PIN].T
     d_cond = thick[slots_all + 2 * PIN :]
-    right = jnp.concatenate(
-        [
-            jnp.concatenate([jnp.zeros((slots_all, PIN), LOW), feat_b, jnp.zeros((slots_all, D + CLASSES), LOW)], 1),
-            jnp.eye(PIN, PIN + FREQ + D + CLASSES, dtype=LOW),
-            jnp.concatenate([jnp.zeros((slots_all, PIN + FREQ), LOW), silu_t_b, onehot], 1),
-        ],
-        0,
-    )
     g_cond = dot(
         jnp.concatenate(thirds(jnp.concatenate([d_hidden, g_patch, d_cond], 0)), 0),
-        jnp.concatenate([right] * 3, 0),
+        right,
         DOWN,
     )
 
     square = lambda g: jnp.sum(g * g)
     sum_at = at_way.finish()
-    split_sq = square(sum_fc1) + square(sum_fc2) + square(sum_at) + square(g_mod)
-    tally = jnp.stack([split_sq + (square(g_head) + square(g_cond)) / n_mp, loss_part[0, 0]])
-    tally = jnp.sum(spread(jnp.broadcast_to(tally[:, None], (2, 128)), ("dp", "mp")), 0)
-    tally = fc1_way.step(fc1_way.step(fc2_way.step(tally)), tally)
-    grad_norm = jnp.sqrt(tally[0, 0])
-    loss_sum = tally[1, 0]
+    parts = [square(g) for g in (sum_fc1, sum_fc2, sum_at, g_mod, g_head, g_cond)] + [loss_part[0, 0]]
+    share = jnp.array([1.0] * 4 + [1.0 / n_mp] * 2 + [1.0], F32)
+    tally = jnp.pad(jnp.stack(parts) * share, (0, 128 - len(parts)))[None]
+    tally = jnp.sum(spread(tally, ("dp", "mp")), 0)
+    tally = fc1_way.step(fc2_way.step(tally), tally)
+    lane = jnp.arange(128)[None]
+    grad_norm = jnp.sqrt(jnp.sum(jnp.where(lane < 6, tally, 0.0), 1, keepdims=True))
+    loss_sum = jnp.sum(jnp.where(lane == 6, tally, 0.0))
     coef = jnp.minimum(1.0, CLIP / (grad_norm + 1e-06))
 
-    halves_of = lambda way: [g.reshape(n_dp // 2, rows, -1) for g in way.finish()]
-    all_fc2 = halves_of(fc2_way)
-    all_fc1 = halves_of(fc1_way)
-    factor = coef[None]
+    all_fc2 = fc2_way.finish()
+    all_fc1 = fc1_way.finish()
+    factor = coef.reshape(1)
     all_at = jnp.broadcast_to(sum_at.astype(LOW)[None], (n_dp,) + sum_at.shape)
     all_at = exchange(after(all_at, factor), "dp")
     span = 8 * width
@@ -931,12 +955,19 @@
     both = lax.cond(near == 0, lambda: both, one_fc1)
     last = lax.cond(near == 0, one_qkv, one_out)
     both = after(both, last)
-    new_weights, new_moms = finish(
+    new_moms = by_rows(
+        momenta_kernel,
+        "momenta",
+        after(factor, last),
+        (sum_at, sum_fc1, sum_fc2, g_mod),
+        (mom_qkv, mom_out, mom_fc1, mom_fc2, mom_mod),
+    )
+    new_weights = by_rows(
+        weights_kernel,
+        "weights",
         near[None],
-        factor,
-        (both[0], swap(both[1], "dp", 1), last[0], swap(last[1], "dp", 1), sum_at, sum_fc1, sum_fc2, g_mod),
+        (both[0], swap(both[1], "dp", 1), last[0], swap(last[1], "dp", 1)),
         (w_qkv, w_out, w_fc1, w_fc2, w_mod),
-        (mom_qkv, mom_out, mom_fc1, mom_fc2, mom_mod),
     )
     coef = after(coef, last)
 
@@ -961,7 +992,7 @@
         adam_out[1][2],
         loss_sum,
         weight_total,
-        grad_norm,
+        grad_norm[0, 0],
     )
 
 

time: 419 us -> 398 us (0.950)
  local copies, waits for them, and re-layouts: 51.9 us -> 33.3 us
  starting transfers between devices: 80.7 us -> 91.4 us
  waiting for transfers between devices: 119 us -> 111 us
    unnamed x307 -> x211, local copies, waits for them, and re-layouts: 37.3 us -> 15.9 us
    ppermute x46 -> x48, starting transfers between devices: 52.8 us -> 65.8 us  [swap(): return lax.ppermute(x, axis, [(i, i ^ bit) for i in range(size)])]
    concatenate x6 -> x2, other arithmetic: 6.42 us -> 1.84 us  [gather_steps(): x = jnp.concatenate([x, other], 0)]
    ppermute x46 -> x48, waiting for transfers between devices: 94 us -> 92.4 us  [swap(): return lax.ppermute(x, axis, [(i, i ^ bit) for i in range(size)])]
  transfers between devices with their start and end apart: 53 -> 55, of which waited for: 25 -> 24; matrix products, arithmetic and copies ran while one was open for 12% -> 14% of each run, Pallas kernels for 14% -> 17%
where the time goes in v1:
time: 398 us; the launch traced here: 391 us
  waiting for transfers between devices  111 us (28%)
  starting transfers between devices  91.4 us (23%)
  Pallas kernels  83.2 us (21%)
  local copies, waits for them, and re-layouts  33.3 us (8%)
  other arithmetic  31.8 us (8%)
  between operations  23 us (6%)
  blocking collectives  10.9 us (3%)
  matrix products  6.63 us (2%)
    ppermute x48, waiting for transfers between devices, swap(): return lax.ppermute(x, axis, [(i, i ^ bit) for i in range(size)])  92.4 us
    ppermute x48, starting transfers between devices, swap(): return lax.ppermute(x, axis, [(i, i ^ bit) for i in range(size)])  65.8 us
    pallas_call x2, Pallas kernels, muon_rows(): pl.pallas_call(functools.partial(muon_kernel, columns, span), grid=(1,),...  42.9 us
    pallas_call x13, Pallas kernels, call(): pl.pallas_call(kernel, out_shape=[jax.ShapeDtypeStruct(*o) for o in outs]...  35.7 us
    all_to_all x5, starting transfers between devices, exchange(): return lax.all_to_all(x, axis, 0, 0, tiled=True)  18 us
    unnamed x211, local copies, waits for them, and re-layouts  15.9 us
    all_to_all x5, waiting for transfers between devices, exchange(): return lax.all_to_all(x, axis, 0, 0, tiled=True)  12.6 us
    all_to_all x1, blocking collectives, spread(): return lax.all_to_all(copies, axis, 0, 0, tiled=True)  10.9 us
  transfers between devices with their start and end apart: 55, of which 24 were waited for; matrix products, arithmetic and copies ran while one was open for 14% of the time, Pallas kernels for 17%

profile of v1, /device:TPU:0, one launch (start us, length us, event | category | flops | bytes accessed | tf_op | source)
XLA Modules:
  0.0 391.4 jit_solution(15024828465894998461)
XLA Ops:
  11.7 7.3 %all-to-all-start = ((bf16[8,112,256]{2,1,0:T(8,128)(2,1)}), bf16[8,112,256]{2,1,0:T(8,128)(2,1)S(1)}, u32[]{:S(2)}, u32[]{:S(2)}) async-start(bf16[8,112,256]{2,1,0:T(8,128)(2,1)} %broadcast_in_dim.186), calls=%async_computation | async-start | bytes 917504 | tf_op jit(solution)/shard_map/all_to_all | solution.py:175
  26.4 5.7 %all-to-all-done = bf16[8,112,256]{2,1,0:T(8,128)(2,1)S(1)} async-done(((bf16[8,112,256]{2,1,0:T(8,128)(2,1)}), bf16[8,112,256]{2,1,0:T(8,128)(2,1)S(1)}, u32[]{:S(2)}, u32[]{:S(2)}) %all-to-all-start) | async-done | bytes 458784 | tf_op jit(solution)/shard_map/all_to_all | solution.py:175
  41.3 4.7 %all-to-all-start.1 = ((f32[8,4,1536]{2,1,0:T(4,128)}), f32[8,4,1536]{2,1,0:T(4,128)S(1)}, u32[]{:S(2)}, u32[]{:S(2)}) async-start(f32[8,4,1536]{2,1,0:T(4,128)} %reshape.503), calls=%async_computation.1 | async-start | bytes 393216 | tf_op jit(solution)/shard_map/all_to_all | solution.py:179
  65.9 6.3 %collective-permute-done.2 = bf16[192,768]{1,0:T(8,128)(2,1)S(1)} collective-permute-done((bf16[192,768]{1,0:T(8,128)(2,1)S(1)}, bf16[192,768]{1,0:T(8,128)(2,1)S(1)}, u32[]{:S(2)}, u32[]{:S(2)}) %collective-permute-start.2) | collective-permute-done | bytes 294944 | tf_op jit(solution)/shard_map/ppermute | solution.py:53
  77.6 6.2 %collective-permute-done.4.h2_ref.h2 = bf16[256,768]{1,0:T(8,128)(2,1)S(1)} collective-permute-done((bf16[256,768]{1,0:T(8,128)(2,1)S(1)}, bf16[256,768]{1,0:T(8,128)(2,1)S(1)}, u32[]{:S(2)}, u32[]{:S(2)}) %collective-permute-start.4) | collective-permute-done | bytes 393248 | tf_op jit(solution)/shard_map/ppermute | solution.py:53
  83.8 6.4 %collective-permute-done.6 = bf16[96,1536]{1,0:T(8,128)(2,1)S(1)} collective-permute-done((bf16[96,1536]{1,0:T(8,128)(2,1)S(1)}, bf16[96,1536]{1,0:T(8,128)(2,1)S(1)}, u32[]{:S(2)}, u32[]{:S(2)}) %collective-permute-start.6) | collective-permute-done | bytes 294944 | tf_op jit(solution)/shard_map/ppermute | solution.py:53
  92.3 8.4 %attend.1 = (bf16[1024,576]{1,0:T(8,128)(2,1)S(1)}, f32[8,1024]{1,0:T(8,128)S(1)}, bf16[1024,192]{1,0:T(8,128)(2,1)S(1)}, f32[2,256,768]{2,1,0:T(8,128)S(1)}, bf16[2,256,768]{2,1,0:T(8,128)(2,1)}) custom-call(s32[1]{0:T(128)} %bitcast.1.single_ref, bf16[256,768]{1,0:T(8,128)(2,1)S(1)} %enter.1.h0_ref.h0, ...), custom_call_target="tpu_custom_call" | custom-call | flops 1 | bytes 1 | tf_op jit(solution)/shard_map/attend/pallas_call | solution.py:247
  111.0 10.5 %collective-permute-done.10.far_ref = bf16[256,768]{1,0:T(8,128)(2,1)S(1)} collective-permute-done((bf16[256,768]{1,0:T(8,128)(2,1)S(1)}, bf16[256,768]{1,0:T(8,128)(2,1)S(1)}, u32[]{:S(2)}, u32[]{:S(2)}) %collective-permute-start.10) | collective-permute-done | bytes 393248 | tf_op jit(solution)/shard_map/ppermute | solution.py:53
  123.8 9.7 %collective-permute-done.12.h2 = bf16[256,768]{1,0:T(8,128)(2,1)S(1)} collective-permute-done((bf16[256,768]{1,0:T(8,128)(2,1)S(1)}, bf16[256,768]{1,0:T(8,128)(2,1)S(1)}, u32[]{:S(2)}, u32[]{:S(2)}) %collective-permute-start.12) | collective-permute-done | bytes 393248 | tf_op jit(solution)/shard_map/ppermute | solution.py:53
  142.5 10.5 %collective-permute-done.16.far_ref = bf16[256,768]{1,0:T(8,128)(2,1)S(1)} collective-permute-done((bf16[256,768]{1,0:T(8,128)(2,1)S(1)}, bf16[256,768]{1,0:T(8,128)(2,1)S(1)}, u32[]{:S(2)}, u32[]{:S(2)}) %collective-permute-start.16) | collective-permute-done | bytes 393248 | tf_op jit(solution)/shard_map/ppermute | solution.py:53
  157.2 9.7 %collective-permute-done.18.d2.h2 = bf16[256,768]{1,0:T(8,128)(2,1)S(1)} collective-permute-done((bf16[256,768]{1,0:T(8,128)(2,1)S(1)}, bf16[256,768]{1,0:T(8,128)(2,1)S(1)}, u32[]{:S(2)}, u32[]{:S(2)}) %collective-permute-start.18) | collective-permute-done | bytes 393248 | tf_op jit(solution)/shard_map/ppermute | solution.py:53
  182.2 6.3 %collective-permute-done.24.far_ref = bf16[256,768]{1,0:T(8,128)(2,1)S(1)} collective-permute-done((bf16[256,768]{1,0:T(8,128)(2,1)S(1)}, bf16[256,768]{1,0:T(8,128)(2,1)S(1)}, u32[]{:S(2)}, u32[]{:S(2)}) %collective-permute-start.24) | collective-permute-done | bytes 393248 | tf_op jit(solution)/shard_map/ppermute | solution.py:53
  193.9 6.8 %collective-permute-start.29 = (bf16[192,768]{1,0:T(8,128)(2,1)S(1)}, bf16[192,768]{1,0:T(8,128)(2,1)S(1)}, u32[]{:S(2)}, u32[]{:S(2)}) collective-permute-start(bf16[192,768]{1,0:T(8,128)(2,1)S(1)} %slice.615), channel_id=1, source_target_pairs={{0,8},{4,12},{8,0},{12,4},{16,24},{20,28},{24,16},{28,20},{1,9},{5... | collective-permute-start | bytes 884744 | tf_op jit(solution)/shard_map/ppermute | solution.py:53
  205.7 6.8 %collective-permute-start.22 = (bf16[192,768]{1,0:T(8,128)(2,1)S(1)}, bf16[192,768]{1,0:T(8,128)(2,1)S(1)}, u32[]{:S(2)}, u32[]{:S(2)}) collective-permute-start(bf16[192,768]{1,0:T(8,128)(2,1)S(1)} %slice.616), channel_id=1, source_target_pairs={{0,8},{4,12},{8,0},{12,4},{16,24},{20,28},{24,16},{28,20},{1,9},{5... | collective-permute-start | bytes 884744 | tf_op jit(solution)/shard_map/ppermute | solution.py:53
  214.7 7.0 %attend_back.1 = (bf16[1024,576]{1,0:T(8,128)(2,1)S(1)}, f32[2,256,768]{2,1,0:T(8,128)S(1)}, bf16[2,256,768]{2,1,0:T(8,128)(2,1)S(1)}) custom-call(s32[1]{0:T(128)} %bitcast.1.single_ref, bf16[1024,576]{1,0:T(8,128)(2,1)S(1)} %copy-done.17, f32[8,1024]{1,0:T(8,128)S(1)} %get-tuple-element.242.total_ref, bf16[256,768]{1,0:T(8,128)(2,1)S(1)} %get-tuple-element.248.d0_ref.d0, ...), custom_call_target="tpu_custom_call" | custom-call | flops 1 | bytes 1 | tf_op jit(solution)/shard_map/attend_back/pallas_call | solution.py:247
  229.6 6.3 %collective-permute-start.32 = (bf16[384,768]{1,0:T(8,128)(2,1)}, bf16[384,768]{1,0:T(8,128)(2,1)}, u32[]{:S(2)}, u32[]{:S(2)}) collective-permute-start(bf16[384,768]{1,0:T(8,128)(2,1)} %get-tuple-element.262), channel_id=1, source_target_pairs={{0,4},{4,0},{8,12},{12,8},{16,20},{20,16},{24,28},{28,24},{1,5},{5... | collective-permute-start | bytes 1769480 | tf_op jit(solution)/shard_map/ppermute | solution.py:53
  240.6 6.3 %collective-permute-start.40 = (bf16[192,768]{1,0:T(8,128)(2,1)}, bf16[192,768]{1,0:T(8,128)(2,1)}, u32[]{:S(2)}, u32[]{:S(2)}) collective-permute-start(bf16[192,768]{1,0:T(8,128)(2,1)} %pad_maximum_fusion.4), channel_id=1, source_target_pairs={{0,4},{4,0},{8,12},{12,8},{16,20},{20,16},{24,28},{28,24},{1,5},{5... | collective-permute-start | bytes 884744 | tf_op jit(solution)/shard_map/ppermute | solution.py:53
  258.3 9.7 %all-to-all-done.3 = f32[32,8,192]{2,1,0:T(8,128)S(1)} async-done(((f32[32,8,192]{2,1,0:T(8,128)}), f32[32,8,192]{2,1,0:T(8,128)S(1)}, u32[]{:S(2)}, u32[]{:S(2)}) %all-to-all-start.3) | async-done | bytes 196640 | tf_op jit(solution)/shard_map/all_to_all | solution.py:179
  283.8 4.2 %collective-permute-done.35 = bf16[192,768]{1,0:T(8,128)(2,1)} collective-permute-done((bf16[192,768]{1,0:T(8,128)(2,1)S(1)}, bf16[192,768]{1,0:T(8,128)(2,1)}, u32[]{:S(2)}, u32[]{:S(2)}) %collective-permute-start.35) | collective-permute-done | bytes 294944 | tf_op jit(solution)/shard_map/ppermute | solution.py:53
  305.4 10.9 %all_to_all.35 = f32[32,1,128]{2,1,0:T(1,128)S(1)} all-to-all(f32[32,1,128]{2,1,0:T(1,128)S(1)} %broadcast_in_dim.209), channel_id=1, replica_groups=mesh['dp'=8,'mp'=4] {'dp','mp'}, dimensions={0} | all-to-all | bytes 32768 | tf_op jit(solution)/shard_map/all_to_all | solution.py:175
  324.4 28.1 %conditional.3 = (bf16[2,96,1536]{2,1,0:T(8,128)(2,1)S(1)}) conditional(s32[]{:T(128)} %convert_element_type.251, (s32[8]{0:T(128)S(1)}, f32[1]{0:T(128)}, f32[5,3]{1,0:T(8,128)S(1)}, bf16[4,2,96,2304]{3,2,1,0:T(8,128)(2,1)}, bf16[192,768]{1,0:T(8,128)(2,1)}, /*index=5*/bf16[192,768]{1,0:T(8,128)(2,1)}, bf16[192,768]{1,0:T(8,128)(2,1)}, ...), branch_computations={%region_20.21_spmd, %region_21.22_spmd} | conditional | flops 1 | bytes 884747 | solution.py:954
  325.4 26.9 %muon.6 = bf16[2,96,1536]{2,1,0:T(8,128)(2,1)S(1)} custom-call(s32[8]{0:T(128)S(1)} %get-tuple-element.84.order_ref, f32[1]{0:T(128)} %get-tuple-element.85.coef_ref, f32[5,3]{1,0:T(8,128)S(1)} %get-tuple-element.86.plan_ref, bf16[4,2,96,2304]{3,2,1,0:T(8,128)(2,1)} %get-tuple-element.300, bf16[4,2,96,32]{3,2,1,0:T(8,128)(2,1)S(1)} %slice.441.refs_0_, ...), custom_call_target="tpu_custom_call" | custom-call | flops 1 | bytes 1 | tf_op jit(solution)/shard_map/cond/branch_1_fun/muon/pallas_call | solution.py:595
  352.5 16.3 %conditional.5 = (bf16[2,96,576]{2,1,0:T(8,128)(2,1)S(1)}) conditional(s32[]{:T(128)} %convert_element_type.251, (s32[8]{0:T(128)S(1)}, f32[1]{0:T(128)}, f32[5,3]{1,0:T(8,128)S(1)}, bf16[4,2,96,2304]{3,2,1,0:T(8,128)(2,1)}, bf16[8,96,768]{2,1,0:T(8,128)(2,1)S(1)}) %tuple.217, (s32[8]{0:T(128)S(1)}, f32[1]{0:T(128)}, f32[5,3]{1,0:T(8,128)S(1)}, ...), branch_computations={%region_24.25_spmd, %region_25.26_spmd} | conditional | flops 1 | bytes 294923 | solution.py:956
  352.5 16.1 %muon.9 = bf16[2,96,576]{2,1,0:T(8,128)(2,1)S(1)} custom-call(s32[8]{0:T(128)S(1)} %get-tuple-element.104.order_ref, f32[1]{0:T(128)} %get-tuple-element.105.coef_ref, f32[5,3]{1,0:T(8,128)S(1)} %get-tuple-element.106.plan_ref, bf16[4,2,96,2304]{3,2,1,0:T(8,128)(2,1)} %get-tuple-element.107.mom_ref, bf16[8,96,768]{2,1,0:T(8,128)(2,1)S(1)} %get-tuple-element.108.refs_0_), custom_call_target="tpu_custom_call" | custom-call | flops 1 | bytes 1 | tf_op jit(solution)/shard_map/cond/branch_1_fun/muon/pallas_call | solution.py:595
  (530 shorter events, 175.4 us)
Async XLA Ops:
  11.7 20.4 %all-to-all-start = ((bf16[8,112,256]{2,1,0:T(8,128)(2,1)}), bf16[8,112,256]{2,1,0:T(8,128)(2,1)S(1)}, u32[]{:S(2)}, u32[]{:S(2)}) async-start(bf16[8,112,256]{2,1,0:T(8,128)(2,1)} %broadcast_in_dim.186), calls=%async_computation | async-start | bytes 917504 | tf_op jit(solution)/shard_map/all_to_all | solution.py:175
  37.8 18.1 %collective-permute-start = (bf16[96,768]{1,0:T(8,128)(2,1)S(1)}, bf16[96,768]{1,0:T(8,128)(2,1)}, u32[]{:S(2)}, u32[]{:S(2)}) collective-permute-start(bf16[96,768]{1,0:T(8,128)(2,1)S(1)} %pad_maximum_fusion.7), channel_id=1, source_target_pairs={{0,16},{4,20},{8,24},{12,28},{16,0},{20,4},{24,8},{28,12},{1,17},{... | collective-permute-start | bytes 442376 | tf_op jit(solution)/shard_map/ppermute | solution.py:53
  41.3 15.5 %all-to-all-start.1 = ((f32[8,4,1536]{2,1,0:T(4,128)}), f32[8,4,1536]{2,1,0:T(4,128)S(1)}, u32[]{:S(2)}, u32[]{:S(2)}) async-start(f32[8,4,1536]{2,1,0:T(4,128)} %reshape.503), calls=%async_computation.1 | async-start | bytes 393216 | tf_op jit(solution)/shard_map/all_to_all | solution.py:179
  47.9 17.7 %collective-permute-start.1 = (bf16[96,2304]{1,0:T(8,128)(2,1)S(1)}, bf16[96,2304]{1,0:T(8,128)(2,1)}, u32[]{:S(2)}, u32[]{:S(2)}) collective-permute-start(bf16[96,2304]{1,0:T(8,128)(2,1)S(1)} %get-tuple-element.217), channel_id=1, source_target_pairs={{0,4},{4,0},{8,12},{12,8},{16,20},{20,16},{24,28},{28,24},{1,5},{5... | collective-permute-start | bytes 1327112 | tf_op jit(solution)/shard_map/ppermute | solution.py:53
  60.9 129.4 %all-gather.3.cloned.1.call-start = ((), (), s32[]{:S(2)}) async-start(), calls=%async_computation.7 | async-start | bytes 4423680 | tf_op jit(solution)/shard_map/all_gather | solution.py:794
  72.9 18.6 %collective-permute-start.7 = (bf16[384,768]{1,0:T(8,128)(2,1)S(1)}, bf16[384,768]{1,0:T(8,128)(2,1)S(1)}, u32[]{:S(2)}, u32[]{:S(2)}) collective-permute-start(bf16[384,768]{1,0:T(8,128)(2,1)S(1)} %get-tuple-element.470), channel_id=1, source_target_pairs={{0,4},{4,0},{8,12},{12,8},{16,20},{20,16},{24,28},{28,24},{1,5},{5... | collective-permute-start | bytes 1769480 | tf_op jit(solution)/shard_map/ppermute | solution.py:53
  107.6 28.4 %collective-permute-start.14 = (bf16[384,1536]{1,0:T(8,128)(2,1)S(1)}, bf16[384,1536]{1,0:T(8,128)(2,1)S(1)}, u32[]{:S(2)}, u32[]{:S(2)}) collective-permute-start(bf16[384,1536]{1,0:T(8,128)(2,1)S(1)} %get-tuple-element.456), channel_id=1, source_target_pairs={{0,4},{4,0},{8,12},{12,8},{16,20},{20,16},{24,28},{28,24},{1,5},{5... | collective-permute-start | bytes 3538952 | tf_op jit(solution)/shard_map/ppermute | solution.py:53
  176.1 16.5 %collective-permute-start.26 = (bf16[384,768]{1,0:T(8,128)(2,1)}, bf16[384,768]{1,0:T(8,128)(2,1)}, u32[]{:S(2)}, u32[]{:S(2)}) collective-permute-start(bf16[384,768]{1,0:T(8,128)(2,1)} %get-tuple-element.250), channel_id=1, source_target_pairs={{0,4},{4,0},{8,12},{12,8},{16,20},{20,16},{24,28},{28,24},{1,5},{5... | collective-permute-start | bytes 1769480 | tf_op jit(solution)/shard_map/ppermute | solution.py:53
  181.6 22.9 %collective-permute-start.21 = (bf16[384,768]{1,0:T(8,128)(2,1)}, bf16[384,768]{1,0:T(8,128)(2,1)}, u32[]{:S(2)}, u32[]{:S(2)}) collective-permute-start(bf16[384,768]{1,0:T(8,128)(2,1)} %get-tuple-element.240), channel_id=1, source_target_pairs={{0,4},{4,0},{8,12},{12,8},{16,20},{20,16},{24,28},{28,24},{1,5},{5... | collective-permute-start | bytes 1769480 | tf_op jit(solution)/shard_map/ppermute | solution.py:53
  190.3 22.2 %collective-permute-start.27 = (bf16[256,768]{1,0:T(8,128)(2,1)S(1)}, bf16[256,768]{1,0:T(8,128)(2,1)S(1)}, u32[]{:S(2)}, u32[]{:S(2)}) collective-permute-start(bf16[256,768]{1,0:T(8,128)(2,1)S(1)} %get-tuple-element.248.d0_ref.d0), channel_id=1, source_target_pairs={{0,2},{1,3},{2,0},{3,1},{4,6},{5,7},{6,4},{7,5},{8,10},{9,11},{10,... | collective-permute-start | bytes 1179656 | tf_op jit(solution)/shard_map/ppermute | solution.py:53
  191.0 23.7 %collective-permute-start.25 = (bf16[256,768]{1,0:T(8,128)(2,1)S(1)}, bf16[256,768]{1,0:T(8,128)(2,1)S(1)}, u32[]{:S(2)}, u32[]{:S(2)}) collective-permute-start(bf16[256,768]{1,0:T(8,128)(2,1)S(1)} %get-tuple-element.248.d0_ref.d0), channel_id=1, source_target_pairs={{0,1},{1,0},{2,3},{3,2},{4,5},{5,4},{6,7},{7,6},{8,9},{9,8},{10,11... | collective-permute-start | bytes 1179656 | tf_op jit(solution)/shard_map/ppermute | solution.py:53
  193.9 18.6 %collective-permute-start.29 = (bf16[192,768]{1,0:T(8,128)(2,1)S(1)}, bf16[192,768]{1,0:T(8,128)(2,1)S(1)}, u32[]{:S(2)}, u32[]{:S(2)}) collective-permute-start(bf16[192,768]{1,0:T(8,128)(2,1)S(1)} %slice.615), channel_id=1, source_target_pairs={{0,8},{4,12},{8,0},{12,4},{16,24},{20,28},{24,16},{28,20},{1,9},{5... | collective-permute-start | bytes 884744 | tf_op jit(solution)/shard_map/ppermute | solution.py:53
  205.7 16.4 %collective-permute-start.22 = (bf16[192,768]{1,0:T(8,128)(2,1)S(1)}, bf16[192,768]{1,0:T(8,128)(2,1)S(1)}, u32[]{:S(2)}, u32[]{:S(2)}) collective-permute-start(bf16[192,768]{1,0:T(8,128)(2,1)S(1)} %slice.616), channel_id=1, source_target_pairs={{0,8},{4,12},{8,0},{12,4},{16,24},{20,28},{24,16},{28,20},{1,9},{5... | collective-permute-start | bytes 884744 | tf_op jit(solution)/shard_map/ppermute | solution.py:53
  222.3 24.6 %collective-permute-start.23 = (bf16[96,768]{1,0:T(8,128)(2,1)S(1)}, bf16[96,768]{1,0:T(8,128)(2,1)S(1)}, u32[]{:S(2)}, u32[]{:S(2)}) collective-permute-start(bf16[96,768]{1,0:T(8,128)(2,1)S(1)} %slice.619), channel_id=1, source_target_pairs={{0,16},{4,20},{8,24},{12,28},{16,0},{20,4},{24,8},{28,12},{1,17},{... | collective-permute-start | bytes 442376 | tf_op jit(solution)/shard_map/ppermute | solution.py:53
  226.1 25.5 %collective-permute-start.33 = (bf16[256,768]{1,0:T(8,128)(2,1)S(1)}, bf16[256,768]{1,0:T(8,128)(2,1)S(1)}, u32[]{:S(2)}, u32[]{:S(2)}) collective-permute-start(bf16[256,768]{1,0:T(8,128)(2,1)S(1)} %fusion.4), channel_id=1, source_target_pairs={{0,2},{1,3},{2,0},{3,1},{4,6},{5,7},{6,4},{7,5},{8,10},{9,11},{10,... | collective-permute-start | bytes 1179656 | tf_op jit(solution)/shard_map/ppermute | solution.py:53
  229.6 28.6 %collective-permute-start.32 = (bf16[384,768]{1,0:T(8,128)(2,1)}, bf16[384,768]{1,0:T(8,128)(2,1)}, u32[]{:S(2)}, u32[]{:S(2)}) collective-permute-start(bf16[384,768]{1,0:T(8,128)(2,1)} %get-tuple-element.262), channel_id=1, source_target_pairs={{0,4},{4,0},{8,12},{12,8},{16,20},{20,16},{24,28},{28,24},{1,5},{5... | collective-permute-start | bytes 1769480 | tf_op jit(solution)/shard_map/ppermute | solution.py:53
  239.8 48.2 %collective-permute-start.39 = (bf16[192,768]{1,0:T(8,128)(2,1)}, bf16[192,768]{1,0:T(8,128)(2,1)}, u32[]{:S(2)}, u32[]{:S(2)}) collective-permute-start(bf16[192,768]{1,0:T(8,128)(2,1)} %pad_maximum_fusion.4), channel_id=1, source_target_pairs={{0,8},{4,12},{8,0},{12,4},{16,24},{20,28},{24,16},{28,20},{1,9},{5... | collective-permute-start | bytes 884744 | tf_op jit(solution)/shard_map/ppermute | solution.py:53
  240.6 47.4 %collective-permute-start.40 = (bf16[192,768]{1,0:T(8,128)(2,1)}, bf16[192,768]{1,0:T(8,128)(2,1)}, u32[]{:S(2)}, u32[]{:S(2)}) collective-permute-start(bf16[192,768]{1,0:T(8,128)(2,1)} %pad_maximum_fusion.4), channel_id=1, source_target_pairs={{0,4},{4,0},{8,12},{12,8},{16,20},{20,16},{24,28},{28,24},{1,5},{5... | collective-permute-start | bytes 884744 | tf_op jit(solution)/shard_map/ppermute | solution.py:53
  247.6 25.5 %collective-permute-start.38 = (bf16[96,768]{1,0:T(8,128)(2,1)}, bf16[96,768]{1,0:T(8,128)(2,1)}, u32[]{:S(2)}, u32[]{:S(2)}) collective-permute-start(bf16[96,768]{1,0:T(8,128)(2,1)} %get-tuple-element.447), channel_id=1, source_target_pairs={{0,16},{4,20},{8,24},{12,28},{16,0},{20,4},{24,8},{28,12},{1,17},{... | collective-permute-start | bytes 442376 | tf_op jit(solution)/shard_map/ppermute | solution.py:53
  289.9 26.4 %collective-permute-start.43 = (bf16[192,768]{1,0:T(8,128)(2,1)}, bf16[192,768]{1,0:T(8,128)(2,1)}, u32[]{:S(2)}, u32[]{:S(2)}) collective-permute-start(bf16[192,768]{1,0:T(8,128)(2,1)} %pad_maximum_fusion.5), channel_id=1, source_target_pairs={{0,8},{4,12},{8,0},{12,4},{16,24},{20,28},{24,16},{28,20},{1,9},{5... | collective-permute-start | bytes 884744 | tf_op jit(solution)/shard_map/ppermute | solution.py:53
  291.0 25.3 %collective-permute-start.44 = (bf16[192,768]{1,0:T(8,128)(2,1)}, bf16[192,768]{1,0:T(8,128)(2,1)S(1)}, u32[]{:S(2)}, u32[]{:S(2)}) collective-permute-start(bf16[192,768]{1,0:T(8,128)(2,1)} %pad_maximum_fusion.5), channel_id=1, source_target_pairs={{0,4},{4,0},{8,12},{12,8},{16,20},{20,16},{24,28},{28,24},{1,5},{5... | collective-permute-start | bytes 884744 | tf_op jit(solution)/shard_map/ppermute | solution.py:53
  292.4 23.8 %collective-permute-start.42 = (bf16[192,768]{1,0:T(8,128)(2,1)}, bf16[192,768]{1,0:T(8,128)(2,1)}, u32[]{:S(2)}, u32[]{:S(2)}) collective-permute-start(bf16[192,768]{1,0:T(8,128)(2,1)} %collective-permute-done.39), channel_id=1, source_target_pairs={{0,4},{4,0},{8,12},{12,8},{16,20},{20,16},{24,28},{28,24},{1,5},{5... | collective-permute-start | bytes 884744 | tf_op jit(solution)/shard_map/ppermute | solution.py:53
  318.8 33.7 %all-to-all-start.6 = ((bf16[8,96,768]{2,1,0:T(8,128)(2,1)}), bf16[8,96,768]{2,1,0:T(8,128)(2,1)S(1)}, u32[]{:S(2)}, u32[]{:S(2)}) async-start(bf16[8,96,768]{2,1,0:T(8,128)(2,1)} %broadcast_in_dim.211), calls=%async_computation.6 | async-start | bytes 2359296 | tf_op jit(solution)/shard_map/all_to_all | solution.py:179
  322.5 30.0 %collective-permute-start.45 = (bf16[192,768]{1,0:T(8,128)(2,1)}, bf16[192,768]{1,0:T(8,128)(2,1)}, u32[]{:S(2)}, u32[]{:S(2)}) collective-permute-start(bf16[192,768]{1,0:T(8,128)(2,1)} %collective-permute-done.43), channel_id=1, source_target_pairs={{0,4},{4,0},{8,12},{12,8},{16,20},{20,16},{24,28},{28,24},{1,5},{5... | collective-permute-start | bytes 884744 | tf_op jit(solution)/shard_map/ppermute | solution.py:53
  (118 other events, 930.3 us)
Sparse Core Ops, SparseCore 0:
  104.5 75.7 all-gather.2

commit v2 on v1

--- a/solution.py
+++ b/solution.py
@@ -925,8 +925,7 @@
     all_fc2 = fc2_way.finish()
     all_fc1 = fc1_way.finish()
     factor = coef.reshape(1)
-    all_at = jnp.broadcast_to(sum_at.astype(LOW)[None], (n_dp,) + sum_at.shape)
-    all_at = exchange(after(all_at, factor), "dp")
+    all_at = lax.all_gather(sum_at.astype(LOW), "dp", axis=0)
     span = 8 * width
 
     silu_c_all = old[:, :, :, 11 * width : 11 * width + slots_all]

time: 398 us -> 390 us (0.980)
  starting transfers between devices: 91.4 us -> 75.9 us
  waiting for transfers between devices: 111 us -> 121 us
    ppermute x48, waiting for transfers between devices: 92.4 us -> 106 us  [swap(): return lax.ppermute(x, axis, [(i, i ^ bit) for i in range(size)])]
    ppermute x48, starting transfers between devices: 65.8 us -> 53.5 us  [swap(): return lax.ppermute(x, axis, [(i, i ^ bit) for i in range(size)])]
    all_to_all x5 -> x4, starting transfers between devices: 18 us -> 14.8 us  [exchange(): return lax.all_to_all(x, axis, 0, 0, tiled=True)]
    all_to_all x5 -> x4, waiting for transfers between devices: 12.6 us -> 9.75 us  [exchange(): return lax.all_to_all(x, axis, 0, 0, tiled=True)]
    unnamed x211 -> x235, local copies, waits for them, and re-layouts: 15.9 us -> 16.8 us
  transfers between devices with their start and end apart: 55 -> 55, of which waited for: 24 -> 27; matrix products, arithmetic and copies ran while one was open for 14% -> 14% of each run, Pallas kernels for 17% -> 17%
where the time goes in v2:
time: 390 us; the launch traced here: 384 us
  waiting for transfers between devices  121 us (31%)
  Pallas kernels  83.8 us (21%)
  starting transfers between devices  75.9 us (19%)
  local copies, waits for them, and re-layouts  32.8 us (8%)
  other arithmetic  29.9 us (8%)
  between operations  23.3 us (6%)
  blocking collectives  10 us (3%)
  matrix products  6.59 us (2%)
    ppermute x48, waiting for transfers between devices, swap(): return lax.ppermute(x, axis, [(i, i ^ bit) for i in range(size)])  106 us
    ppermute x48, starting transfers between devices, swap(): return lax.ppermute(x, axis, [(i, i ^ bit) for i in range(size)])  53.5 us
    pallas_call x2, Pallas kernels, muon_rows(): pl.pallas_call(functools.partial(muon_kernel, columns, span), grid=(1,),...  43.3 us
    pallas_call x13, Pallas kernels, call(): pl.pallas_call(kernel, out_shape=[jax.ShapeDtypeStruct(*o) for o in outs]...  35.8 us
    unnamed x235, local copies, waits for them, and re-layouts  16.8 us
    all_to_all x4, starting transfers between devices, exchange(): return lax.all_to_all(x, axis, 0, 0, tiled=True)  14.8 us
    all_to_all x1, blocking collectives, spread(): return lax.all_to_all(copies, axis, 0, 0, tiled=True)  10 us
    all_to_all x4, waiting for transfers between devices, exchange(): return lax.all_to_all(x, axis, 0, 0, tiled=True)  9.75 us
  transfers between devices with their start and end apart: 55, of which 27 were waited for; matrix products, arithmetic and copies ran while one was open for 14% of the time, Pallas kernels for 17%

profile of v2, /device:TPU:0, one launch (start us, length us, event | category | flops | bytes accessed | tf_op | source)
XLA Modules:
  0.0 384.1 jit_solution(7812462753996605275)
XLA Ops:
  11.7 7.3 %all-to-all-start = ((bf16[8,112,256]{2,1,0:T(8,128)(2,1)}), bf16[8,112,256]{2,1,0:T(8,128)(2,1)S(1)}, u32[]{:S(2)}, u32[]{:S(2)}) async-start(bf16[8,112,256]{2,1,0:T(8,128)(2,1)} %broadcast_in_dim.180), calls=%async_computation | async-start | bytes 917504 | tf_op jit(solution)/shard_map/all_to_all | solution.py:175
  26.4 5.7 %all-to-all-done = bf16[8,112,256]{2,1,0:T(8,128)(2,1)S(1)} async-done(((bf16[8,112,256]{2,1,0:T(8,128)(2,1)}), bf16[8,112,256]{2,1,0:T(8,128)(2,1)S(1)}, u32[]{:S(2)}, u32[]{:S(2)}) %all-to-all-start) | async-done | bytes 458784 | tf_op jit(solution)/shard_map/all_to_all | solution.py:175
  41.3 4.7 %all-to-all-start.1 = ((f32[8,4,1536]{2,1,0:T(4,128)}), f32[8,4,1536]{2,1,0:T(4,128)S(1)}, u32[]{:S(2)}, u32[]{:S(2)}) async-start(f32[8,4,1536]{2,1,0:T(4,128)} %reshape.502), calls=%async_computation.1 | async-start | bytes 393216 | tf_op jit(solution)/shard_map/all_to_all | solution.py:179
  65.9 6.3 %collective-permute-done.2 = bf16[192,768]{1,0:T(8,128)(2,1)S(1)} collective-permute-done((bf16[192,768]{1,0:T(8,128)(2,1)S(1)}, bf16[192,768]{1,0:T(8,128)(2,1)S(1)}, u32[]{:S(2)}, u32[]{:S(2)}) %collective-permute-start.2) | collective-permute-done | bytes 294944 | tf_op jit(solution)/shard_map/ppermute | solution.py:53
  77.6 6.2 %collective-permute-done.4.h2_ref.h2 = bf16[256,768]{1,0:T(8,128)(2,1)S(1)} collective-permute-done((bf16[256,768]{1,0:T(8,128)(2,1)S(1)}, bf16[256,768]{1,0:T(8,128)(2,1)S(1)}, u32[]{:S(2)}, u32[]{:S(2)}) %collective-permute-start.4) | collective-permute-done | bytes 393248 | tf_op jit(solution)/shard_map/ppermute | solution.py:53
  83.8 6.4 %collective-permute-done.6 = bf16[96,1536]{1,0:T(8,128)(2,1)S(1)} collective-permute-done((bf16[96,1536]{1,0:T(8,128)(2,1)S(1)}, bf16[96,1536]{1,0:T(8,128)(2,1)S(1)}, u32[]{:S(2)}, u32[]{:S(2)}) %collective-permute-start.6) | collective-permute-done | bytes 294944 | tf_op jit(solution)/shard_map/ppermute | solution.py:53
  92.3 8.2 %attend.1 = (bf16[1024,576]{1,0:T(8,128)(2,1)S(1)}, f32[8,1024]{1,0:T(8,128)S(1)}, bf16[1024,192]{1,0:T(8,128)(2,1)S(1)}, f32[2,256,768]{2,1,0:T(8,128)S(1)}, bf16[2,256,768]{2,1,0:T(8,128)(2,1)}) custom-call(s32[1]{0:T(128)} %bitcast.1.single_ref, bf16[256,768]{1,0:T(8,128)(2,1)S(1)} %enter.1.h0_ref.h0, ...), custom_call_target="tpu_custom_call" | custom-call | flops 1 | bytes 1 | tf_op jit(solution)/shard_map/attend/pallas_call | solution.py:247
  107.4 6.9 %collective-permute-start.14 = (bf16[384,1536]{1,0:T(8,128)(2,1)S(1)}, bf16[384,1536]{1,0:T(8,128)(2,1)S(1)}, u32[]{:S(2)}, u32[]{:S(2)}) collective-permute-start(bf16[384,1536]{1,0:T(8,128)(2,1)S(1)} %get-tuple-element.454), channel_id=1, source_target_pairs={{0,4},{4,0},{8,12},{12,8},{16,20},{20,16},{24,28},{28,24},{1,5},{5... | collective-permute-start | bytes 3538952 | tf_op jit(solution)/shard_map/ppermute | solution.py:53
  116.1 10.5 %collective-permute-done.10.far_ref = bf16[256,768]{1,0:T(8,128)(2,1)S(1)} collective-permute-done((bf16[256,768]{1,0:T(8,128)(2,1)S(1)}, bf16[256,768]{1,0:T(8,128)(2,1)S(1)}, u32[]{:S(2)}, u32[]{:S(2)}) %collective-permute-start.10) | collective-permute-done | bytes 393248 | tf_op jit(solution)/shard_map/ppermute | solution.py:53
  129.0 9.8 %collective-permute-done.12.h2 = bf16[256,768]{1,0:T(8,128)(2,1)S(1)} collective-permute-done((bf16[256,768]{1,0:T(8,128)(2,1)S(1)}, bf16[256,768]{1,0:T(8,128)(2,1)S(1)}, u32[]{:S(2)}, u32[]{:S(2)}) %collective-permute-start.12) | collective-permute-done | bytes 393248 | tf_op jit(solution)/shard_map/ppermute | solution.py:53
  147.4 10.5 %collective-permute-done.16.far_ref = bf16[256,768]{1,0:T(8,128)(2,1)S(1)} collective-permute-done((bf16[256,768]{1,0:T(8,128)(2,1)S(1)}, bf16[256,768]{1,0:T(8,128)(2,1)S(1)}, u32[]{:S(2)}, u32[]{:S(2)}) %collective-permute-start.16) | collective-permute-done | bytes 393248 | tf_op jit(solution)/shard_map/ppermute | solution.py:53
  162.2 9.7 %collective-permute-done.18.d2.h2 = bf16[256,768]{1,0:T(8,128)(2,1)S(1)} collective-permute-done((bf16[256,768]{1,0:T(8,128)(2,1)S(1)}, bf16[256,768]{1,0:T(8,128)(2,1)S(1)}, u32[]{:S(2)}, u32[]{:S(2)}) %collective-permute-start.18) | collective-permute-done | bytes 393248 | tf_op jit(solution)/shard_map/ppermute | solution.py:53
  187.1 6.6 %collective-permute-done.24.far_ref = bf16[256,768]{1,0:T(8,128)(2,1)S(1)} collective-permute-done((bf16[256,768]{1,0:T(8,128)(2,1)S(1)}, bf16[256,768]{1,0:T(8,128)(2,1)S(1)}, u32[]{:S(2)}, u32[]{:S(2)}) %collective-permute-start.24) | collective-permute-done | bytes 393248 | tf_op jit(solution)/shard_map/ppermute | solution.py:53
  200.7 8.7 %collective-permute-done.21 = bf16[384,768]{1,0:T(8,128)(2,1)} collective-permute-done((bf16[384,768]{1,0:T(8,128)(2,1)}, bf16[384,768]{1,0:T(8,128)(2,1)}, u32[]{:S(2)}, u32[]{:S(2)}) %collective-permute-start.21) | collective-permute-done | bytes 589856 | tf_op jit(solution)/shard_map/ppermute | solution.py:53
  214.6 7.0 %attend_back.1 = (bf16[1024,576]{1,0:T(8,128)(2,1)S(1)}, f32[2,256,768]{2,1,0:T(8,128)S(1)}, bf16[2,256,768]{2,1,0:T(8,128)(2,1)S(1)}) custom-call(s32[1]{0:T(128)} %bitcast.1.single_ref, bf16[1024,576]{1,0:T(8,128)(2,1)S(1)} %copy-done.17, f32[8,1024]{1,0:T(8,128)S(1)} %get-tuple-element.241.total_ref, bf16[256,768]{1,0:T(8,128)(2,1)S(1)} %get-tuple-element.247.d0_ref.d0, ...), custom_call_target="tpu_custom_call" | custom-call | flops 1 | bytes 1 | tf_op jit(solution)/shard_map/attend_back/pallas_call | solution.py:247
  222.2 7.7 %collective-permute-start.23 = (bf16[96,768]{1,0:T(8,128)(2,1)S(1)}, bf16[96,768]{1,0:T(8,128)(2,1)S(1)}, u32[]{:S(2)}, u32[]{:S(2)}) collective-permute-start(bf16[96,768]{1,0:T(8,128)(2,1)S(1)} %slice.619), channel_id=1, source_target_pairs={{0,16},{4,20},{8,24},{12,28},{16,0},{20,4},{24,8},{28,12},{1,17},{... | collective-permute-start | bytes 442376 | tf_op jit(solution)/shard_map/ppermute | solution.py:53
  236.3 4.5 %collective-permute-done.23 = bf16[96,768]{1,0:T(8,128)(2,1)S(1)} collective-permute-done((bf16[96,768]{1,0:T(8,128)(2,1)S(1)}, bf16[96,768]{1,0:T(8,128)(2,1)S(1)}, u32[]{:S(2)}, u32[]{:S(2)}) %collective-permute-start.23) | collective-permute-done | bytes 147488 | tf_op jit(solution)/shard_map/ppermute | solution.py:53
  253.4 7.1 %all-to-all-done.3 = f32[32,8,192]{2,1,0:T(8,128)S(1)} async-done(((f32[32,8,192]{2,1,0:T(8,128)}), f32[32,8,192]{2,1,0:T(8,128)S(1)}, u32[]{:S(2)}, u32[]{:S(2)}) %all-to-all-start.3) | async-done | bytes 196640 | tf_op jit(solution)/shard_map/all_to_all | solution.py:179
  281.4 7.1 %collective-permute-done.36 = bf16[96,768]{1,0:T(8,128)(2,1)S(1)} collective-permute-done((bf16[96,768]{1,0:T(8,128)(2,1)S(1)}, bf16[96,768]{1,0:T(8,128)(2,1)S(1)}, u32[]{:S(2)}, u32[]{:S(2)}) %collective-permute-start.36) | collective-permute-done | bytes 147488 | tf_op jit(solution)/shard_map/ppermute | solution.py:53
  304.1 10.0 %all_to_all.30 = f32[32,1,128]{2,1,0:T(1,128)S(1)} all-to-all(f32[32,1,128]{2,1,0:T(1,128)S(1)} %broadcast_in_dim.203), channel_id=1, replica_groups=mesh['dp'=8,'mp'=4] {'dp','mp'}, dimensions={0} | all-to-all | bytes 32768 | tf_op jit(solution)/shard_map/all_to_all | solution.py:175
  316.1 28.1 %conditional.3 = (bf16[2,96,1536]{2,1,0:T(8,128)(2,1)S(1)}) conditional(s32[]{:T(128)} %convert_element_type.251, (s32[8]{0:T(128)S(1)}, f32[1]{0:T(128)}, f32[5,3]{1,0:T(8,128)S(1)}, bf16[4,2,96,2304]{3,2,1,0:T(8,128)(2,1)}, bf16[192,768]{1,0:T(8,128)(2,1)S(1)}, /*index=5*/bf16[192,768]{1,0:T(8,128)(2,1)S(1)}, bf16[192,768]{1,0:T(8,128)(2,1)}, ...), branch_computations={%region_20.21_spmd, %region_21.22_spmd} | conditional | flops 1 | bytes 884747 | solution.py:953
  317.2 26.8 %muon.6 = bf16[2,96,1536]{2,1,0:T(8,128)(2,1)S(1)} custom-call(s32[8]{0:T(128)S(1)} %get-tuple-element.84.order_ref, f32[1]{0:T(128)} %get-tuple-element.85.coef_ref, f32[5,3]{1,0:T(8,128)S(1)} %get-tuple-element.86.plan_ref, bf16[4,2,96,2304]{3,2,1,0:T(8,128)(2,1)} %get-tuple-element.298, bf16[4,2,96,32]{3,2,1,0:T(8,128)(2,1)S(1)} %slice.441.refs_0_, ...), custom_call_target="tpu_custom_call" | custom-call | flops 1 | bytes 1 | tf_op jit(solution)/shard_map/cond/branch_1_fun/muon/pallas_call | solution.py:595
  344.3 16.7 %conditional.5 = (bf16[2,96,576]{2,1,0:T(8,128)(2,1)S(1)}) conditional(s32[]{:T(128)} %convert_element_type.251, (s32[8]{0:T(128)S(1)}, f32[1]{0:T(128)}, f32[5,3]{1,0:T(8,128)S(1)}, bf16[4,2,96,2304]{3,2,1,0:T(8,128)(2,1)}, bf16[8,96,768]{2,1,0:T(8,128)(2,1)}) %tuple.218, (s32[8]{0:T(128)S(1)}, f32[1]{0:T(128)}, f32[5,3]{1,0:T(8,128)S(1)}, ...), branch_computations={%region_24.25_spmd, %region_25.26_spmd} | conditional | flops 1 | bytes 294923 | solution.py:955
  344.3 16.4 %muon.9 = bf16[2,96,576]{2,1,0:T(8,128)(2,1)S(1)} custom-call(s32[8]{0:T(128)S(1)} %get-tuple-element.104.order_ref, f32[1]{0:T(128)} %get-tuple-element.105.coef_ref, f32[5,3]{1,0:T(8,128)S(1)} %get-tuple-element.106.plan_ref, bf16[4,2,96,2304]{3,2,1,0:T(8,128)(2,1)} %get-tuple-element.107.mom_ref, bf16[8,96,768]{2,1,0:T(8,128)(2,1)} %get-tuple-element.108.refs_0_), custom_call_target="tpu_custom_call" | custom-call | flops 1 | bytes 1 | tf_op jit(solution)/shard_map/cond/branch_1_fun/muon/pallas_call | solution.py:595
  (554 shorter events, 166.0 us)
Async XLA Ops:
  11.7 20.4 %all-to-all-start = ((bf16[8,112,256]{2,1,0:T(8,128)(2,1)}), bf16[8,112,256]{2,1,0:T(8,128)(2,1)S(1)}, u32[]{:S(2)}, u32[]{:S(2)}) async-start(bf16[8,112,256]{2,1,0:T(8,128)(2,1)} %broadcast_in_dim.180), calls=%async_computation | async-start | bytes 917504 | tf_op jit(solution)/shard_map/all_to_all | solution.py:175
  37.8 18.1 %collective-permute-start = (bf16[96,768]{1,0:T(8,128)(2,1)S(1)}, bf16[96,768]{1,0:T(8,128)(2,1)}, u32[]{:S(2)}, u32[]{:S(2)}) collective-permute-start(bf16[96,768]{1,0:T(8,128)(2,1)S(1)} %pad_maximum_fusion.7), channel_id=1, source_target_pairs={{0,16},{4,20},{8,24},{12,28},{16,0},{20,4},{24,8},{28,12},{1,17},{... | collective-permute-start | bytes 442376 | tf_op jit(solution)/shard_map/ppermute | solution.py:53
  41.3 15.4 %all-to-all-start.1 = ((f32[8,4,1536]{2,1,0:T(4,128)}), f32[8,4,1536]{2,1,0:T(4,128)S(1)}, u32[]{:S(2)}, u32[]{:S(2)}) async-start(f32[8,4,1536]{2,1,0:T(4,128)} %reshape.502), calls=%async_computation.1 | async-start | bytes 393216 | tf_op jit(solution)/shard_map/all_to_all | solution.py:179
  47.9 17.7 %collective-permute-start.1 = (bf16[96,2304]{1,0:T(8,128)(2,1)S(1)}, bf16[96,2304]{1,0:T(8,128)(2,1)}, u32[]{:S(2)}, u32[]{:S(2)}) collective-permute-start(bf16[96,2304]{1,0:T(8,128)(2,1)S(1)} %get-tuple-element.216), channel_id=1, source_target_pairs={{0,4},{4,0},{8,12},{12,8},{16,20},{20,16},{24,28},{28,24},{1,5},{5... | collective-permute-start | bytes 1327112 | tf_op jit(solution)/shard_map/ppermute | solution.py:53
  60.9 134.9 %all-gather.5.cloned.1.call-start = ((), (), s32[]{:S(2)}) async-start(), calls=%async_computation.6 | async-start | bytes 4423680 | tf_op jit(solution)/shard_map/all_gather | solution.py:794
  72.9 18.6 %collective-permute-start.7 = (bf16[384,768]{1,0:T(8,128)(2,1)S(1)}, bf16[384,768]{1,0:T(8,128)(2,1)S(1)}, u32[]{:S(2)}, u32[]{:S(2)}) collective-permute-start(bf16[384,768]{1,0:T(8,128)(2,1)S(1)} %get-tuple-element.468), channel_id=1, source_target_pairs={{0,4},{4,0},{8,12},{12,8},{16,20},{20,16},{24,28},{28,24},{1,5},{5... | collective-permute-start | bytes 1769480 | tf_op jit(solution)/shard_map/ppermute | solution.py:53
  74.9 15.3 %collective-permute-start.6 = (bf16[96,1536]{1,0:T(8,128)(2,1)S(1)}, bf16[96,1536]{1,0:T(8,128)(2,1)S(1)}, u32[]{:S(2)}, u32[]{:S(2)}) collective-permute-start(bf16[96,1536]{1,0:T(8,128)(2,1)S(1)} %pad_maximum_fusion.3), channel_id=1, source_target_pairs={{0,16},{4,20},{8,24},{12,28},{16,0},{20,4},{24,8},{28,12},{1,17},{... | collective-permute-start | bytes 884744 | tf_op jit(solution)/shard_map/ppermute | solution.py:53
  77.6 13.9 %collective-permute-start.3 = (bf16[256,768]{1,0:T(8,128)(2,1)S(1)}, bf16[256,768]{1,0:T(8,128)(2,1)S(1)}, u32[]{:S(2)}, u32[]{:S(2)}) collective-permute-start(bf16[256,768]{1,0:T(8,128)(2,1)S(1)} %enter.1.h0_ref.h0), channel_id=1, source_target_pairs={{0,1},{1,0},{2,3},{3,2},{4,5},{5,4},{6,7},{7,6},{8,9},{9,8},{10,11... | collective-permute-start | bytes 1179656 | tf_op jit(solution)/shard_map/ppermute | solution.py:53
  91.1 15.1 %collective-permute-start.9 = (bf16[192,1536]{1,0:T(8,128)(2,1)}, bf16[192,1536]{1,0:T(8,128)(2,1)}, u32[]{:S(2)}, u32[]{:S(2)}) collective-permute-start(bf16[192,1536]{1,0:T(8,128)(2,1)} %pad_maximum_fusion.1), channel_id=1, source_target_pairs={{0,8},{4,12},{8,0},{12,4},{16,24},{20,28},{24,16},{28,20},{1,9},{5... | collective-permute-start | bytes 1769480 | tf_op jit(solution)/shard_map/ppermute | solution.py:53
  107.4 33.6 %collective-permute-start.14 = (bf16[384,1536]{1,0:T(8,128)(2,1)S(1)}, bf16[384,1536]{1,0:T(8,128)(2,1)S(1)}, u32[]{:S(2)}, u32[]{:S(2)}) collective-permute-start(bf16[384,1536]{1,0:T(8,128)(2,1)S(1)} %get-tuple-element.454), channel_id=1, source_target_pairs={{0,4},{4,0},{8,12},{12,8},{16,20},{20,16},{24,28},{28,24},{1,5},{5... | collective-permute-start | bytes 3538952 | tf_op jit(solution)/shard_map/ppermute | solution.py:53
  181.1 16.5 %collective-permute-start.26 = (bf16[384,768]{1,0:T(8,128)(2,1)}, bf16[384,768]{1,0:T(8,128)(2,1)}, u32[]{:S(2)}, u32[]{:S(2)}) collective-permute-start(bf16[384,768]{1,0:T(8,128)(2,1)} %get-tuple-element.249), channel_id=1, source_target_pairs={{0,4},{4,0},{8,12},{12,8},{16,20},{20,16},{24,28},{28,24},{1,5},{5... | collective-permute-start | bytes 1769480 | tf_op jit(solution)/shard_map/ppermute | solution.py:53
  186.8 22.6 %collective-permute-start.21 = (bf16[384,768]{1,0:T(8,128)(2,1)}, bf16[384,768]{1,0:T(8,128)(2,1)}, u32[]{:S(2)}, u32[]{:S(2)}) collective-permute-start(bf16[384,768]{1,0:T(8,128)(2,1)} %get-tuple-element.239), channel_id=1, source_target_pairs={{0,4},{4,0},{8,12},{12,8},{16,20},{20,16},{24,28},{28,24},{1,5},{5... | collective-permute-start | bytes 1769480 | tf_op jit(solution)/shard_map/ppermute | solution.py:53
  195.8 16.6 %collective-permute-start.27 = (bf16[256,768]{1,0:T(8,128)(2,1)S(1)}, bf16[256,768]{1,0:T(8,128)(2,1)S(1)}, u32[]{:S(2)}, u32[]{:S(2)}) collective-permute-start(bf16[256,768]{1,0:T(8,128)(2,1)S(1)} %get-tuple-element.247.d0_ref.d0), channel_id=1, source_target_pairs={{0,2},{1,3},{2,0},{3,1},{4,6},{5,7},{6,4},{7,5},{8,10},{9,11},{10,... | collective-permute-start | bytes 1179656 | tf_op jit(solution)/shard_map/ppermute | solution.py:53
  196.5 18.1 %collective-permute-start.25 = (bf16[256,768]{1,0:T(8,128)(2,1)S(1)}, bf16[256,768]{1,0:T(8,128)(2,1)S(1)}, u32[]{:S(2)}, u32[]{:S(2)}) collective-permute-start(bf16[256,768]{1,0:T(8,128)(2,1)S(1)} %get-tuple-element.247.d0_ref.d0), channel_id=1, source_target_pairs={{0,1},{1,0},{2,3},{3,2},{4,5},{5,4},{6,7},{7,6},{8,9},{9,8},{10,11... | collective-permute-start | bytes 1179656 | tf_op jit(solution)/shard_map/ppermute | solution.py:53
  222.2 18.7 %collective-permute-start.23 = (bf16[96,768]{1,0:T(8,128)(2,1)S(1)}, bf16[96,768]{1,0:T(8,128)(2,1)S(1)}, u32[]{:S(2)}, u32[]{:S(2)}) collective-permute-start(bf16[96,768]{1,0:T(8,128)(2,1)S(1)} %slice.619), channel_id=1, source_target_pairs={{0,16},{4,20},{8,24},{12,28},{16,0},{20,4},{24,8},{28,12},{1,17},{... | collective-permute-start | bytes 442376 | tf_op jit(solution)/shard_map/ppermute | solution.py:53
  236.3 15.1 %collective-permute-start.32 = (bf16[384,768]{1,0:T(8,128)(2,1)}, bf16[384,768]{1,0:T(8,128)(2,1)}, u32[]{:S(2)}, u32[]{:S(2)}) collective-permute-start(bf16[384,768]{1,0:T(8,128)(2,1)} %get-tuple-element.261), channel_id=1, source_target_pairs={{0,4},{4,0},{8,12},{12,8},{16,20},{20,16},{24,28},{28,24},{1,5},{5... | collective-permute-start | bytes 1769480 | tf_op jit(solution)/shard_map/ppermute | solution.py:53
  246.5 14.0 %all-to-all-start.3 = ((f32[32,8,192]{2,1,0:T(8,128)}), f32[32,8,192]{2,1,0:T(8,128)S(1)}, u32[]{:S(2)}, u32[]{:S(2)}) async-start(f32[32,8,192]{2,1,0:T(8,128)} %bitcast.59), calls=%async_computation.3 | async-start | bytes 524288 | tf_op jit(solution)/shard_map/all_to_all | solution.py:179
  266.6 77.7 %all-gather.7.cloned.1.call-start = ((), (), s32[]{:S(2)}) async-start(), calls=%async_computation.7 | async-start | bytes 1327104 | tf_op jit(solution)/shard_map/all_gather | solution.py:928
  266.7 24.5 %collective-permute-start.39 = (bf16[192,768]{1,0:T(8,128)(2,1)S(1)}, bf16[192,768]{1,0:T(8,128)(2,1)S(1)}, u32[]{:S(2)}, u32[]{:S(2)}) collective-permute-start(bf16[192,768]{1,0:T(8,128)(2,1)S(1)} %pad_maximum_fusion.4), channel_id=1, source_target_pairs={{0,8},{4,12},{8,0},{12,4},{16,24},{20,28},{24,16},{28,20},{1,9},{5... | collective-permute-start | bytes 884744 | tf_op jit(solution)/shard_map/ppermute | solution.py:53
  268.7 22.6 %collective-permute-start.40 = (bf16[192,768]{1,0:T(8,128)(2,1)S(1)}, bf16[192,768]{1,0:T(8,128)(2,1)}, u32[]{:S(2)}, u32[]{:S(2)}) collective-permute-start(bf16[192,768]{1,0:T(8,128)(2,1)S(1)} %pad_maximum_fusion.4), channel_id=1, source_target_pairs={{0,4},{4,0},{8,12},{12,8},{16,20},{20,16},{24,28},{28,24},{1,5},{5... | collective-permute-start | bytes 884744 | tf_op jit(solution)/shard_map/ppermute | solution.py:53
  294.7 19.5 %collective-permute-start.43 = (bf16[192,768]{1,0:T(8,128)(2,1)S(1)}, bf16[192,768]{1,0:T(8,128)(2,1)S(1)}, u32[]{:S(2)}, u32[]{:S(2)}) collective-permute-start(bf16[192,768]{1,0:T(8,128)(2,1)S(1)} %pad_maximum_fusion.5), channel_id=1, source_target_pairs={{0,8},{4,12},{8,0},{12,4},{16,24},{20,28},{24,16},{28,20},{1,9},{5... | collective-permute-start | bytes 884744 | tf_op jit(solution)/shard_map/ppermute | solution.py:53
  294.7 20.1 %collective-permute-start.44 = (bf16[192,768]{1,0:T(8,128)(2,1)S(1)}, bf16[192,768]{1,0:T(8,128)(2,1)}, u32[]{:S(2)}, u32[]{:S(2)}) collective-permute-start(bf16[192,768]{1,0:T(8,128)(2,1)S(1)} %pad_maximum_fusion.5), channel_id=1, source_target_pairs={{0,4},{4,0},{8,12},{12,8},{16,20},{20,16},{24,28},{28,24},{1,5},{5... | collective-permute-start | bytes 884744 | tf_op jit(solution)/shard_map/ppermute | solution.py:53
  295.7 19.0 %collective-permute-start.42 = (bf16[192,768]{1,0:T(8,128)(2,1)S(1)}, bf16[192,768]{1,0:T(8,128)(2,1)}, u32[]{:S(2)}, u32[]{:S(2)}) collective-permute-start(bf16[192,768]{1,0:T(8,128)(2,1)S(1)} %collective-permute-done.39), channel_id=1, source_target_pairs={{0,4},{4,0},{8,12},{12,8},{16,20},{20,16},{24,28},{28,24},{1,5},{5... | collective-permute-start | bytes 884744 | tf_op jit(solution)/shard_map/ppermute | solution.py:53
  314.1 30.1 %collective-permute-start.45 = (bf16[192,768]{1,0:T(8,128)(2,1)S(1)}, bf16[192,768]{1,0:T(8,128)(2,1)S(1)}, u32[]{:S(2)}, u32[]{:S(2)}) collective-permute-start(bf16[192,768]{1,0:T(8,128)(2,1)S(1)} %collective-permute-done.43), channel_id=1, source_target_pairs={{0,4},{4,0},{8,12},{12,8},{16,20},{20,16},{24,28},{28,24},{1,5},{5... | collective-permute-start | bytes 884744 | tf_op jit(solution)/shard_map/ppermute | solution.py:53
  (130 other events, 959.8 us)
Sparse Core Ops, SparseCore 0:
  104.3 74.8 all-gather.4
  289.4 45.3 all-gather.6
